TPU v7x, 32 devices: a whole 2x2x4 slice. The times are simulated.
32 devices in a mesh: groups: 2 (over y), seq: 16 (over z, x, core).
Axes of the slice: x: 2, y: 2, z: 4, core: 2. Of those that a mesh axis runs over, the one named last changes fastest.
Arguments:
- tokens: bfloat16 [4096, 256], P(('groups', 'seq')), parts along dimension 0, may hold values from -6 to 6
- inv_rms_a: float32 [4096], P(('groups', 'seq')), parts along dimension 0, may hold values from 0.5 to 2
- gain_a: float32 [256], replicated, may hold values from 0.1 to 1.9
- proj_a: bfloat16 [256, 768], replicated, may hold values from -0.375 to 0.375
- taps_a: bfloat16 [128, 256], replicated, may hold values from -0.5 to 0.5
- out_a: bfloat16 [256, 256], replicated, may hold values from -0.375 to 0.375
- inv_rms_b: float32 [4096], P(('groups', 'seq')), parts along dimension 0, may hold values from 0.5 to 2
- gain_b: float32 [256], replicated, may hold values from 0.1 to 1.9
- proj_b: bfloat16 [256, 768], replicated, may hold values from -0.375 to 0.375
- rates_b: float32 [16, 256], replicated, may hold values from 1.4648438e-06 to 0.033
- residues_b: float32 [16, 256], replicated, may hold values from -4 to 4
- out_b: bfloat16 [256, 256], replicated, may hold values from -0.375 to 0.375
Outputs:
- partial_a: bfloat16 [4096, 256], P(('groups', 'seq')), parts along dimension 0
- partial_b: bfloat16 [4096, 256], P(('groups', 'seq')), parts along dimension 0
There are 2 independent parts, one for each index of `groups`. A program takes and returns all parts, laid end to end along the dimension named above; an argument that names none is the same for every part. Nothing has to cross between parts.
All inputs are finite; a program needn't handle non-finite values.
Results may differ from a plain program's by a relative error of at most 0.019.
Values may be sent and summed in bfloat16 or wider, within the bound.
No kernel may reach another device: no remote copies, remote signals or barrier semaphores. Data moves between devices by JAX's collectives and lax.ppermute only.
A program may use at most 64 MiB of HBM per device.

v0:
```python
import math

import jax
import jax.numpy as jnp
from jax import lax
from jax.sharding import PartitionSpec as P

HIGHEST_PREC = lax.Precision.HIGHEST


def from_behind(block, axis, distance):
    devices = range(lax.axis_size(axis))
    route = [(i - distance, i) for i in devices if i - distance in devices]
    return lax.ppermute(block, axis, route)


def rms_scale(values, inv_rms, gain):
    floats = values.astype(jnp.float32)
    return (floats * inv_rms[:, None] * gain).astype(jnp.bfloat16)


def mode_weights(rates, residues, length):
    energy = -jnp.expm1(-2.0 * rates) / -jnp.expm1(-2.0 * rates * length)
    return residues * jnp.sqrt(energy)


def matmul(form, left, right):
    return jnp.einsum(form, left, right, precision=HIGHEST_PREC)


def short_conv(product, rim_part, taps):
    tok_rows, feat_width = product.shape
    extended = jnp.concatenate([rim_part, product], 0)[None]
    kernel = jnp.flip(taps, 0)[:, None, :]
    result = lax.conv_general_dilated(
        extended,
        kernel,
        (1,),
        [(0, 0)],
        dimension_numbers=("NHC", "HIO", "NHC"),
        feature_group_count=feat_width,
        preferred_element_type=jnp.float32,
    )
    return result[0, 1:]


def dft_table(row_count, col_count, modulus):
    row_ids = lax.broadcasted_iota(jnp.int32, (row_count, col_count), 0)
    col_ids = lax.broadcasted_iota(jnp.int32, (row_count, col_count), 1)
    angles = (row_ids * col_ids % modulus).astype(jnp.float32) * (2.0 * math.pi / modulus)
    return (jnp.cos(angles), jnp.sin(angles))


def forward_transform(values, tables):
    cos_outer, sin_outer, cos_twist, sin_twist, cos_inner, sin_inner = tables
    segment_re = matmul("kn,cnq->ckq", cos_outer, values)
    segment_im = -matmul("kn,cnq->ckq", sin_outer, values)
    twist_re = segment_re * cos_twist + segment_im * sin_twist
    twist_im = segment_im * cos_twist - segment_re * sin_twist
    spec_re = matmul("ckn,nm->ckm", twist_re, cos_inner) + matmul(
        "ckn,nm->ckm", twist_im, sin_inner
    )
    spec_im = matmul("ckn,nm->ckm", twist_im, cos_inner) - matmul(
        "ckn,nm->ckm", twist_re, sin_inner
    )
    return (spec_re, spec_im)


def inverse_transform(spec_re, spec_im, tables, fft_len):
    cos_outer, sin_outer, cos_twist, sin_twist, cos_inner, sin_inner = tables
    back_re = matmul("ckn,nm->ckm", spec_re, cos_inner) - matmul("ckn,nm->ckm", spec_im, sin_inner)
    back_im = matmul("ckn,nm->ckm", spec_im, cos_inner) + matmul("ckn,nm->ckm", spec_re, sin_inner)
    turned_re = back_re * cos_twist - back_im * sin_twist
    turned_im = back_im * cos_twist + back_re * sin_twist
    half_rows = cos_outer.shape[1]
    real_part = matmul("kn,ckq->cnq", cos_outer, turned_re) - matmul(
        "kn,ckq->cnq", sin_outer, turned_im
    )
    return real_part / float(fft_len)


def sampled_filter(rates, weights, devices, tok_rows):
    dev_ids = lax.broadcasted_iota(jnp.int32, (devices, tok_rows), 0)
    row_ids = lax.broadcasted_iota(jnp.int32, (devices, tok_rows), 1)
    positions = (dev_ids * tok_rows + row_ids).astype(jnp.float32)
    terms = weights[:, :, None, None] * jnp.exp(-rates[:, :, None, None] * positions[None, None])
    return jnp.sum(terms, axis=0)


def spectral_conv(received, rates, residues, devices, tok_rows):
    chan_count = received.shape[0]
    fft_len = 2 * devices * tok_rows
    cos_outer, sin_outer = dft_table(2 * devices, devices, 2 * devices)
    cos_twist, sin_twist = dft_table(2 * devices, tok_rows, fft_len)
    cos_inner, sin_inner = dft_table(tok_rows, tok_rows, tok_rows)
    tables = (cos_outer, sin_outer, cos_twist, sin_twist, cos_inner, sin_inner)
    weights = mode_weights(rates, residues, float(devices * tok_rows))
    data_re, data_im = forward_transform(
        received.astype(jnp.float32).reshape(chan_count, devices, tok_rows), tables
    )
    filt_re, filt_im = forward_transform(sampled_filter(rates, weights, devices, tok_rows), tables)
    prod_re = data_re * filt_re - data_im * filt_im
    prod_im = data_re * filt_im + data_im * filt_re
    return inverse_transform(prod_re, prod_im, tables, fft_len).reshape(
        chan_count, devices * tok_rows
    )


def on_device(
    tokens,
    inv_rms_a,
    gain_a,
    proj_a,
    taps_a,
    out_a,
    inv_rms_b,
    gain_b,
    proj_b,
    rates_b,
    residues_b,
    out_b,
):
    tok_rows, feat_width = tokens.shape
    tap_count = taps_a.shape[0]
    normed = rms_scale(tokens, inv_rms_a, gain_a)
    projected = jnp.dot(normed, proj_a, preferred_element_type=jnp.float32)
    queries = projected[:, :feat_width]
    product = (projected[:, feat_width : 2 * feat_width] * projected[:, 2 * feat_width :]).astype(
        jnp.bfloat16
    )
    rim_part = from_behind(product, "seq", 1)
    short_out = short_conv(product, rim_part, taps_a)
    gated_a = (queries * short_out).astype(jnp.bfloat16)
    partial_a = jnp.dot(gated_a, out_a, preferred_element_type=jnp.float32).astype(jnp.bfloat16)
    hidden = (tokens.astype(jnp.float32) + partial_a.astype(jnp.float32)).astype(jnp.bfloat16)
    normed_b = rms_scale(hidden, inv_rms_b, gain_b)
    projected_b = lax.dot_general(
        proj_b, normed_b, (((0,), (1,)), ((), ())), preferred_element_type=jnp.float32
    )
    queries_b = projected_b[:feat_width]
    signal = (projected_b[feat_width : 2 * feat_width] * projected_b[2 * feat_width :]).astype(
        jnp.bfloat16
    )
    devices = lax.axis_size("seq")
    chan_count = feat_width // devices
    received = lax.all_to_all(signal, "seq", split_axis=0, concat_axis=1, tiled=True)
    offset = lax.axis_index("seq") * chan_count
    local_rates = lax.dynamic_slice_in_dim(rates_b, offset, chan_count, 1)
    residues = lax.dynamic_slice_in_dim(residues_b, offset, chan_count, 1)
    filtered = spectral_conv(received, local_rates, residues, devices, tok_rows).astype(
        jnp.bfloat16
    )
    long_out = lax.all_to_all(filtered, "seq", split_axis=1, concat_axis=0, tiled=True)
    long_out = lax.optimization_barrier(long_out)
    gated_b = (queries_b * long_out.astype(jnp.float32)).astype(jnp.bfloat16)
    partial_b = lax.dot_general(
        gated_b, out_b, (((0,), (0,)), ((), ())), preferred_element_type=jnp.float32
    ).astype(jnp.bfloat16)
    return (partial_a, partial_b)


def solution(mesh):
    placed = (
        P(("groups", "seq"), None),
        P(("groups", "seq")),
        P(),
        P(),
        P(),
        P(),
        P(("groups", "seq")),
        P(),
        P(),
        P(),
        P(),
        P(),
    )
    return jax.shard_map(
        on_device,
        mesh=mesh,
        in_specs=placed,
        out_specs=(P(("groups", "seq"), None), P(("groups", "seq"), None)),
        check_vma=False,
    )
```

profile of v0, /device:TPU:0, one launch (start us, length us, event | category | flops | bytes accessed | tf_op | source)
XLA Modules:
  0.0 44.6 jit_solution(11224540105381886314)
XLA Ops:
  0.7 1.0 %copy-done = bf16[256,768]{1,0:T(8,128)(2,1)S(1)} copy-done((bf16[256,768]{1,0:T(8,128)(2,1)S(1)}, bf16[256,768]{1,0:T(8,128)(2,1)}, u32[]{:S(2)}) %copy-start) | copy-done | bytes 393240
  1.6 1.1 %fusion.36 = f32[128,768]{1,0:T(8,128)S(1)} fusion(bf16[256,768]{1,0:T(8,128)(2,1)S(1)} %copy-done, bf16[128,256]{1,0:T(8,128)(2,1)} %param.12, f32[256]{0:T(256)} %param.14, f32[128]{0:T(128)} %param.13), kind=kOutput, calls=%fused_computation.65 | convolution fusion | flops 50462720 | bytes 853504 | tf_op jit(solution)/shard_map/dot_general | solution.py:126
  2.8 2.4 %collective-permute-start = (bf16[128,256]{1,0:T(8,128)(2,1)S(1)}, bf16[128,256]{1,0:T(8,128)(2,1)S(1)}, u32[]{:S(2)}, u32[]{:S(2)}) collective-permute-start(bf16[128,256]{1,0:T(8,128)(2,1)S(1)} %fusion.19), channel_id=1, source_target_pairs={{0,1},{1,2},{2,3},{3,4},{4,5},{5,6},{6,7},{7,8},{8,9},{9,10},{10,1... | collective-permute-start | bytes 196616 | tf_op jit(solution)/shard_map/ppermute | solution.py:14
  5.4 0.7 %multiply_reduce_fusion = f32[16,16,128]{2,1,0:T(8,128)S(1)} fusion(f32[16,128]{1,0:T(8,128)S(1)} %add_convert_fusion, f32[16,16]{1,0:T(8,128)S(1)} %get-tuple-element.5, f32[16,16]{1,0:T(8,128)S(1)} %get-tuple-element.4), kind=kLoop, calls=%fused_computation | loop fusion | flops 1540096 | bytes 141312 | tf_op jit(solution)/shard_map/reduce_sum | solution.py:87
  6.1 0.5 %fusion = f32[16,32,128]{2,1,0:T(8,128)S(1)} fusion(f32[16,16,128]{2,1,0:T(8,128)S(1)} %multiply_reduce_fusion), kind=kOutput, calls=%fused_computation.9 | convolution fusion | flops 12655616 | bytes 393216 | tf_op jit(solution)/shard_map/kn,cnq->ckq/dot_general | solution.py:28
  6.6 0.5 %convolution_bitcast_fusion.1 = f32[16,32,128]{2,1,0:T(8,128)S(1)} fusion(f32[16,16,128]{2,1,0:T(8,128)S(1)} %multiply_reduce_fusion), kind=kOutput, calls=%fused_computation.10 | convolution fusion | flops 12590080 | bytes 393216 | tf_op jit(solution)/shard_map/kn,cnq->ckq/dot_general | solution.py:28
  7.1 0.6 %fusion.29 = f32[16,32,128]{2,1,0:T(8,128)S(1)} fusion(f32[16,32,128]{2,1,0:T(8,128)S(1)} %convolution_bitcast_fusion.1, f32[16,32,128]{2,1,0:T(8,128)S(1)} %fusion, f32[32,128]{1,0:T(8,128)S(1)} %get-tuple-element.6, f32[32,128]{1,0:T(8,128)S(1)} %get-tuple-element.7), kind=kOutput, calls=%fused_computation.61 | convolution fusion | flops 101089280 | bytes 819200 | tf_op jit(solution)/shard_map/ckn,nm->ckm/dot_general | solution.py:28
  7.7 0.6 %convolution_subtract_fusion.1 = f32[16,32,128]{2,1,0:T(8,128)S(1)} fusion(f32[16,32,128]{2,1,0:T(8,128)S(1)} %fusion.29, f32[16,32,128]{2,1,0:T(8,128)S(1)} %fusion, f32[16,32,128]{2,1,0:T(8,128)S(1)} %convolution_bitcast_fusion.1, f32[32,128]{1,0:T(8,128)S(1)} %get-tuple-element.6, f32[32,128]{1,0:T(8,128)S(1)} %get-tuple-element.7), kind=kOutput, calls=%fused_computation.4 | convolution fusion | flops 101154816 | bytes 1081344 | tf_op jit(solution)/shard_map/ckn,nm->ckm/dot_general | solution.py:28
  8.3 0.6 %fusion.28 = f32[16,32,128]{2,1,0:T(8,128)S(1)} fusion(f32[16,32,128]{2,1,0:T(8,128)S(1)} %fusion, f32[16,32,128]{2,1,0:T(8,128)S(1)} %convolution_bitcast_fusion.1, f32[32,128]{1,0:T(8,128)S(1)} %get-tuple-element.6, f32[32,128]{1,0:T(8,128)S(1)} %get-tuple-element.7), kind=kOutput, calls=%fused_computation.60 | convolution fusion | flops 101089280 | bytes 819200 | tf_op jit(solution)/shard_map/ckn,nm->ckm/dot_general | solution.py:28
  8.9 0.2 copy-done.6
  9.3 2.0 %fusion.5 = f32[1,128,256]{2,0,1:T(1,128)S(1)} fusion(bf16[1,256,256]{2,1,0:T(8,128)(2,1)S(1)} %maximum_bitcast_fusion, bf16[128,1,256]{2,0,1:T(8,128)(2,1)S(1)} %bitcast.80), kind=kOutput, calls=%fused_computation.20 | convolution fusion | flops 8388608 | bytes 327680 | tf_op jit(solution)/shard_map/slice | solution.py:44
  11.5 0.8 %copy-done.1 = bf16[256,768]{1,0:T(8,128)(2,1)S(1)} copy-done((bf16[256,768]{1,0:T(8,128)(2,1)S(1)}, bf16[256,768]{1,0:T(8,128)(2,1)}, u32[]{:S(2)}) %copy-start.1) | copy-done | bytes 393240
  12.3 0.2 convolution_bitcast_fusion
  12.5 0.4 copy-done.3
  12.9 0.7 %copy.32 = bf16[256,128]{1,0:T(8,128)(2,1)} copy(bf16[256,128]{0,1:T(8,128)(2,1)S(1)} %fusion.17) | data formatting | bytes 131072 | tf_op jit(solution)/shard_map/convert_element_type | solution.py:141
  13.7 7.2 %all-to-all-start = ((bf16[16,16,128]{2,1,0:T(8,128)(2,1)}), bf16[16,16,128]{2,1,0:T(8,128)(2,1)S(1)}, u32[]{:S(2)}, u32[]{:S(2)}) async-start(bf16[16,16,128]{2,1,0:T(8,128)(2,1)} %bitcast.3), calls=%async_computation | async-start | bytes 131072 | tf_op jit(solution)/shard_map/all_to_all | solution.py:146
  20.9 0.6 %convolution_add_fusion.1 = f32[16,32,128]{2,1,0:T(8,128)S(1)} fusion(f32[16,32,128]{2,1,0:T(8,128)S(1)} %fusion.28, f32[16,32,128]{2,1,0:T(8,128)S(1)} %convolution_bitcast_fusion.1, f32[16,32,128]{2,1,0:T(8,128)S(1)} %fusion, f32[32,128]{1,0:T(8,128)S(1)} %get-tuple-element.6, f32[32,128]{1,0:T(8,128)S(1)} %get-tuple-element.7), kind=kOutput, calls=%fused_computation.6 | convolution fusion | flops 101154816 | bytes 1081344 | tf_op jit(solution)/shard_map/ckn,nm->ckm/dot_general | solution.py:28
  21.5 6.3 %all-to-all-done = bf16[16,16,128]{2,1,0:T(8,128)(2,1)S(1)} async-done(((bf16[16,16,128]{2,1,0:T(8,128)(2,1)}), bf16[16,16,128]{2,1,0:T(8,128)(2,1)S(1)}, u32[]{:S(2)}, u32[]{:S(2)}) %all-to-all-start) | async-done | bytes 65568 | tf_op jit(solution)/shard_map/all_to_all | solution.py:146
  27.8 0.4 fusion.1
  28.1 0.4 convolution_bitcast_fusion.2
  28.5 0.6 %fusion.27 = f32[16,32,128]{2,1,0:T(8,128)S(1)} fusion(f32[16,32,128]{2,1,0:T(8,128)S(1)} %convolution_bitcast_fusion.2, f32[16,32,128]{2,1,0:T(8,128)S(1)} %fusion.1, f32[32,128]{1,0:T(8,128)S(1)} %get-tuple-element.6, f32[32,128]{1,0:T(8,128)S(1)} %get-tuple-element.7), kind=kOutput, calls=%fused_computation.59 | convolution fusion | flops 101089280 | bytes 819200 | tf_op jit(solution)/shard_map/ckn,nm->ckm/dot_general | solution.py:28
  29.1 0.6 %fusion.26 = f32[16,32,128]{2,1,0:T(8,128)S(1)} fusion(f32[16,32,128]{2,1,0:T(8,128)S(1)} %fusion.1, f32[16,32,128]{2,1,0:T(8,128)S(1)} %convolution_bitcast_fusion.2, f32[32,128]{1,0:T(8,128)S(1)} %get-tuple-element.6, f32[32,128]{1,0:T(8,128)S(1)} %get-tuple-element.7), kind=kOutput, calls=%fused_computation.58 | convolution fusion | flops 101089280 | bytes 819200 | tf_op jit(solution)/shard_map/ckn,nm->ckm/dot_general | solution.py:28
  29.7 0.6 %convolution_add_fusion.2 = f32[16,32,128]{2,1,0:T(8,128)S(1)} fusion(f32[16,32,128]{2,1,0:T(8,128)S(1)} %fusion.26, f32[16,32,128]{2,1,0:T(8,128)S(1)} %convolution_bitcast_fusion.2, f32[16,32,128]{2,1,0:T(8,128)S(1)} %fusion.1, f32[32,128]{1,0:T(8,128)S(1)} %get-tuple-element.6, f32[32,128]{1,0:T(8,128)S(1)} %get-tuple-element.7), kind=kOutput, calls=%fused_computation.7 | convolution fusion | flops 101154816 | bytes 1081344 | tf_op jit(solution)/shard_map/ckn,nm->ckm/dot_general | solution.py:28
  30.4 0.6 %multiply_subtract_fusion = (f32[16,32,128]{2,1,0:T(8,128)S(1)}, f32[16,32,128]{2,1,0:T(8,128)S(1)}) fusion(f32[16,32,128]{2,1,0:T(8,128)S(1)} %convolution_subtract_fusion.1, f32[16,32,128]{2,1,0:T(8,128)S(1)} %convolution_add_fusion.2, f32[16,32,128]{2,1,0:T(8,128)S(1)} %convolution_add_fusion.1, f32[16,32,128]{2,1,0:T(8,128)S(1)} %fusion.27, ...), kind=kOutput, calls=%fused_computation.30 | convolution fusion | flops 101548032 | bytes 2129920 | tf_op jit(solution)/shard_map/ckn,nm->ckm/dot_general | solution.py:28
  31.0 0.6 %fusion.46 = f32[16,32,128]{2,1,0:T(8,128)S(1)} fusion(f32[16,32,128]{2,1,0:T(8,128)S(1)} %get-tuple-element.2), kind=kOutput, calls=%fused_computation.74 | convolution fusion | flops 100892672 | bytes 524288 | tf_op jit(solution)/shard_map/ckn,nm->ckm/dot_general | solution.py:28
  31.6 0.6 %fusion.44 = f32[16,32,128]{2,1,0:T(8,128)S(1)} fusion(f32[16,32,128]{2,1,0:T(8,128)S(1)} %get-tuple-element.3), kind=kOutput, calls=%fused_computation.72 | convolution fusion | flops 100892672 | bytes 524288 | tf_op jit(solution)/shard_map/ckn,nm->ckm/dot_general | solution.py:28
  32.3 0.6 %convolution_subtract_fusion = f32[16,32,128]{2,1,0:T(8,128)S(1)} fusion(f32[16,32,128]{2,1,0:T(8,128)S(1)} %fusion.46, f32[16,32,128]{2,1,0:T(8,128)S(1)} %get-tuple-element.3), kind=kOutput, calls=%fused_computation.3 | convolution fusion | flops 100958208 | bytes 786432 | tf_op jit(solution)/shard_map/ckn,nm->ckm/dot_general | solution.py:28
  32.9 0.6 %convolution_add_fusion = f32[16,32,128]{2,1,0:T(8,128)S(1)} fusion(f32[16,32,128]{2,1,0:T(8,128)S(1)} %fusion.44, f32[16,32,128]{2,1,0:T(8,128)S(1)} %get-tuple-element.2), kind=kOutput, calls=%fused_computation.2 | convolution fusion | flops 100958208 | bytes 786432 | tf_op jit(solution)/shard_map/ckn,nm->ckm/dot_general | solution.py:28
  33.5 0.3 fusion.10
  33.9 0.3 fusion.4
  34.2 9.5 %all_to_all.32 = bf16[16,16,128]{2,0,1:T(8,128)(2,1)S(1)} all-to-all(bf16[16,16,128]{2,0,1:T(8,128)(2,1)S(1)} %copy.34), channel_id=1, replica_groups=mesh['groups'=2,'seq'=16] {'seq'}, dimensions={1} | all-to-all | bytes 131072 | tf_op jit(solution)/shard_map/all_to_all | solution.py:153
  43.8 0.8 %convolution_convert_fusion = bf16[128,256]{1,0:T(8,128)(2,1)} fusion(bf16[256,256]{1,0:T(8,128)(2,1)S(1)} %copy-done.5, f32[768,128]{0,1:T(8,128)S(1)} %convolution_bitcast_fusion, bf16[256,128]{0,1:T(8,128)(2,1)S(1)} %copy.35), kind=kOutput, calls=%fused_computation.17 | convolution fusion | flops 16908288 | bytes 393216 | tf_op jit(solution)/shard_map/dot_general | solution.py:156
  (30 shorter events, 0.7 us)
Async XLA Ops:
  0.6 1.0 %copy-start = (bf16[256,768]{1,0:T(8,128)(2,1)S(1)}, bf16[256,768]{1,0:T(8,128)(2,1)}, u32[]{:S(2)}) copy-start(bf16[256,768]{1,0:T(8,128)(2,1)} %param.15) | copy-start | bytes 1179652
  0.6 4.7 %copy-start.7 = (f32[16,256]{1,0:T(8,128)S(1)}, f32[16,256]{1,0:T(8,128)}, u32[]{:S(2)}) copy-start(f32[16,256]{1,0:T(8,128)} %param.22) | copy-start | bytes 49156
  0.7 4.7 %copy-start.8 = (f32[16,256]{1,0:T(8,128)S(1)}, f32[16,256]{1,0:T(8,128)}, u32[]{:S(2)}) copy-start(f32[16,256]{1,0:T(8,128)} %param.21) | copy-start | bytes 49156
  2.8 6.5 %collective-permute-start = (bf16[128,256]{1,0:T(8,128)(2,1)S(1)}, bf16[128,256]{1,0:T(8,128)(2,1)S(1)}, u32[]{:S(2)}, u32[]{:S(2)}) collective-permute-start(bf16[128,256]{1,0:T(8,128)(2,1)S(1)} %fusion.19), channel_id=1, source_target_pairs={{0,1},{1,2},{2,3},{3,4},{4,5},{5,6},{6,7},{7,8},{8,9},{9,10},{10,1... | collective-permute-start | bytes 196616 | tf_op jit(solution)/shard_map/ppermute | solution.py:14
  8.3 0.8 %copy-start.6 = (bf16[128,256]{1,0:T(8,128)(2,1)S(1)}, bf16[128,256]{1,0:T(8,128)(2,1)}, u32[]{:S(2)}) copy-start(bf16[128,256]{1,0:T(8,128)(2,1)} %param.16) | copy-start | bytes 196612
  9.3 2.0 %copy-start.4 = (bf16[256,256]{1,0:T(8,128)(2,1)S(1)}, bf16[256,256]{1,0:T(8,128)(2,1)}, u32[]{:S(2)}) copy-start(bf16[256,256]{1,0:T(8,128)(2,1)} %param.17) | copy-start | bytes 393220
  9.3 2.2 %copy-start.9 = (f32[256]{0:T(256)S(1)}, f32[256]{0:T(256)}, u32[]{:S(2)}) copy-start(f32[256]{0:T(256)} %param.19) | copy-start | bytes 3076
  9.3 2.2 %copy-start.10 = (f32[128]{0:T(128)S(1)}, f32[128]{0:T(128)}, u32[]{:S(2)}) copy-start(f32[128]{0:T(128)} %param.18) | copy-start | bytes 1540
  11.3 1.0 %copy-start.1 = (bf16[256,768]{1,0:T(8,128)(2,1)S(1)}, bf16[256,768]{1,0:T(8,128)(2,1)}, u32[]{:S(2)}) copy-start(bf16[256,768]{1,0:T(8,128)(2,1)} %param.20) | copy-start | bytes 1179652
  11.3 1.0 %copy-start.2 = (bf16[128,256]{1,0:T(8,128)(2,1)S(1)}, bf16[128,256]{1,0:T(8,128)(2,1)}, u32[]{:S(2)}) copy-start(bf16[128,256]{1,0:T(8,128)(2,1)} %param.12) | copy-start | bytes 196612
  12.3 0.6 %copy-start.3 = (bf16[128,256]{1,0:T(8,128)(2,1)}, bf16[128,256]{1,0:T(8,128)(2,1)S(1)}, u32[]{:S(2)}) copy-start(bf16[128,256]{1,0:T(8,128)(2,1)S(1)} %convolution_convert_fusion.1) | copy-start | bytes 196612
  13.7 14.1 %all-to-all-start = ((bf16[16,16,128]{2,1,0:T(8,128)(2,1)}), bf16[16,16,128]{2,1,0:T(8,128)(2,1)S(1)}, u32[]{:S(2)}, u32[]{:S(2)}) async-start(bf16[16,16,128]{2,1,0:T(8,128)(2,1)} %bitcast.3), calls=%async_computation | async-start | bytes 131072 | tf_op jit(solution)/shard_map/all_to_all | solution.py:146
  33.9 10.0 %copy-start.5 = (bf16[256,256]{1,0:T(8,128)(2,1)S(1)}, bf16[256,256]{1,0:T(8,128)(2,1)}, u32[]{:S(2)}) copy-start(bf16[256,256]{1,0:T(8,128)(2,1)} %param.23) | copy-start | bytes 393220
where the time goes:
time: 45 us; the launch traced here: 44.6 us
  matrix products  14 us (31%)
  starting transfers between devices  9.55 us (21%)
  blocking collectives  9.48 us (21%)
  waiting for transfers between devices  6.28 us (14%)
  local copies, waits for them, and re-layouts  3.35 us (7%)
  other arithmetic  1.02 us (2%)
  between operations  1.02 us (2%)
    dot_general x18, matrix products, matmul(): return jnp.einsum(form, left, right, precision=HIGHEST_PREC)  9.69 us
    all_to_all x1, blocking collectives, on_device(): lax.all_to_all(filtered, 'seq', split_axis=1, concat_axis=0, tiled=True)  9.48 us
    all_to_all x1, starting transfers between devices, on_device(): lax.all_to_all(signal, 'seq', split_axis=0, concat_axis=1, tiled=True)  7.19 us
    all_to_all x1, waiting for transfers between devices, on_device(): lax.all_to_all(signal, 'seq', split_axis=0, concat_axis=1, tiled=True)  6.28 us
    unnamed x22, local copies, waits for them, and re-layouts  2.41 us
    ppermute x1, starting transfers between devices, from_behind(): return lax.ppermute(block, axis, route)  2.36 us
    slice x1, matrix products, short_conv(): return result[0, 1:]  1.96 us
    dot_general x1, matrix products, on_device(): projected = jnp.dot(normed, proj_a, preferred_element_type=jnp.float32)  1.1 us
  transfers between devices with their start and end apart: 2, of which 1 were waited for; matrix products, arithmetic and copies ran while one was open for 10% of the time, Pallas kernels for 0%

commit v1 on v0

v1 whole, which is shorter than its diff:
```python
import functools

import jax
import jax.numpy as jnp
from jax import lax
from jax.experimental import pallas as pl
from jax.experimental.pallas import tpu as pltpu
from jax.sharding import PartitionSpec as P

F32 = jnp.float32
BF16 = jnp.bfloat16
LANES = 128
SUB = 8
TAP_GROUP = 4
STEP = SUB * TAP_GROUP
VMEM_LIMIT = 32 * 1024 * 1024


def call(kernel, outs, scratch=(), flops=0, data=0):
    return pl.pallas_call(
        kernel,
        out_shape=outs,
        out_specs=jax.tree.map(lambda _: pl.BlockSpec(memory_space=pltpu.VMEM), outs),
        scratch_shapes=list(scratch),
        compiler_params=pltpu.CompilerParams(vmem_limit_bytes=VMEM_LIMIT),
        cost_estimate=pl.CostEstimate(flops=flops, bytes_accessed=data, transcendentals=0),
    )


def spread(scales, width):
    rows = scales.shape[1]
    square = jnp.transpose(jnp.broadcast_to(scales, (LANES, rows)))
    return jnp.concatenate([square] * (width // LANES), 1)


def scaled(values, scales, gain):
    return (values * spread(scales, values.shape[1]) * gain).astype(BF16)


def dot(left, right):
    return jnp.dot(left, right, preferred_element_type=F32)


def shifted_copies(values, store, lead):
    rows, width = values.shape
    tail = store.shape[1] - lead - rows
    if tail:
        values = jnp.concatenate([values, jnp.zeros((tail, width), F32)], 0)
    if lead:
        values = jnp.concatenate([jnp.zeros((lead, width), F32), values], 0)
    store[0] = values
    for r in range(1, SUB):
        store[r] = pltpu.roll(values, r, 0)


def tap_sum(taps, store, group, base, size):
    width = store.shape[2]

    def body(step, total):
        first = pl.multiple_of(base - step * SUB, SUB)
        for r in range(SUB):
            tap = taps[pl.ds((group * TAP_GROUP + step) * SUB + r, 1), :]
            total = total + tap * store[r, pl.ds(first, size), :]
        return total

    return lax.fori_loop(0, TAP_GROUP, body, jnp.zeros((size, width), F32))


def own_taps(values, taps, store, total):
    rows = values.shape[0]
    shifted_copies(values, store, STEP)
    total[...] = tap_sum(taps, store, 0, STEP, rows)
    for group in range(1, rows // STEP):
        skip = group * STEP
        total[pl.ds(skip, rows - skip), :] += tap_sum(taps, store, group, STEP, rows - skip)


def rim_taps(values, taps, store, total):
    rows = values.shape[0]
    shifted_copies(values, store, 0)
    for group in range(rows // STEP):
        size = (group + 1) * STEP
        total[pl.ds(0, size), :] += tap_sum(taps, store, group, rows - group * STEP, size)


def first_kernel(tokens, inv_rms, gain, proj, queries, product):
    width = tokens.shape[1]
    normed = scaled(tokens[...].astype(F32), inv_rms[...], gain[...])
    projected = dot(normed, proj[...])
    queries[...] = projected[:, :width]
    product[...] = (projected[:, width : 2 * width] * projected[:, 2 * width :]).astype(BF16)


def near_kernel(product, taps, total, store, taps_wide):
    taps_wide[...] = taps[...].astype(F32)
    own_taps(product[...].astype(F32), taps_wide, store, total)


def middle_kernel(
    near, rim, taps, queries, out_a, tokens, inv_rms, gain, proj, fade, fall,
    partial, signal, queries_b, state, store, taps_wide, total,
):
    width = near.shape[1]
    modes = fade.shape[0]
    taps_wide[...] = taps[...].astype(F32)
    total[...] = near[...]
    rim_taps(rim[...].astype(F32), taps_wide, store, total)
    gated = (queries[...] * total[...]).astype(BF16)
    term = dot(gated, out_a[...]).astype(BF16)
    partial[...] = term
    hidden = (tokens[...].astype(F32) + term.astype(F32)).astype(BF16)
    normed = scaled(hidden.astype(F32), inv_rms[...], gain[...])
    pair = dot(normed, proj[:, width:])
    mixed = (pair[:, :width] * pair[:, width:]).astype(BF16).astype(F32)
    signal[...] = mixed
    for lane in range(0, width, LANES):
        here = slice(lane, lane + LANES)
        for m in range(modes):
            drop = fade[m : m + 1, here]
            held = mixed[:SUB, here]
            for row in range(SUB, mixed.shape[0], SUB):
                held = held * drop + mixed[row : row + SUB, here]
            state[m : m + 1, here] = jnp.sum(held * fall[m, :, here], 0, keepdims=True)
    queries_b[...] = dot(normed, proj[:, :width])


def local_kernel(signal, response, total, store):
    own_taps(signal[...], response, store, total)


def last_kernel(near, carry, rise, fade, queries, out_b, partial):
    rows, width = near.shape
    modes = fade.shape[0]
    columns = []
    for lane in range(0, width, LANES):
        here = slice(lane, lane + LANES)
        sums = [near[row : row + SUB, here] for row in range(0, rows, SUB)]
        for m in range(modes):
            drop = fade[m : m + 1, here]
            held = carry[m : m + 1, here] * rise[m, :, here]
            for i in range(len(sums)):
                sums[i] = sums[i] + held
                if i + 1 < len(sums):
                    held = held * drop
        columns.append(jnp.concatenate(sums, 0))
    long_out = jnp.concatenate(columns, 1).astype(BF16).astype(F32)
    gated = (queries[...] * long_out).astype(BF16)
    partial[...] = dot(gated, out_b[...]).astype(BF16)


def mode_weights(rates, residues, length):
    energy = -jnp.expm1(-2.0 * rates) / -jnp.expm1(-2.0 * rates * length)
    return residues * jnp.sqrt(energy)


def levels(devices):
    found, stride = [], 1
    while stride < devices:
        radix = 4 if devices // stride % 4 == 0 else 2
        found.append((stride, radix))
        stride *= radix
    assert stride == devices
    return found


def swap(block, devices, mask):
    return lax.ppermute(block, "seq", [(i, i ^ mask) for i in range(devices)])


def decay(rates, count, keep=True):
    count = jnp.maximum(count, 0).astype(F32)
    return jnp.where(keep, jnp.exp(-rates * count), 0.0)


def states_before(state, rates, rows, devices):
    me = lax.axis_index("seq")
    before = jnp.zeros_like(state)
    total = state
    for stride, radix in levels(devices):
        place = me // stride % radix
        parts = [total] + [swap(total, devices, k * stride) for k in range(1, radix)]
        summed = jnp.zeros_like(state)
        for k, part in enumerate(parts):
            other = place ^ k
            gap = ((place - 1 - other) * stride + me % stride) * rows
            before = before + part * decay(rates, gap, other < place)
            summed = summed + part * decay(rates, (radix - 1 - other) * stride * rows)
        total = summed
    return before


def on_device(
    tokens,
    inv_rms_a,
    gain_a,
    proj_a,
    taps_a,
    out_a,
    inv_rms_b,
    gain_b,
    proj_b,
    rates_b,
    residues_b,
    out_b,
):
    rows, width = tokens.shape
    taps = taps_a.shape[0]
    modes = rates_b.shape[0]
    devices = lax.axis_size("seq")
    assert taps == rows and rows % STEP == 0
    wide = jax.ShapeDtypeStruct((rows, width), F32)
    narrow = jax.ShapeDtypeStruct((rows, width), BF16)
    own_store = pltpu.VMEM((SUB, rows + STEP, width), F32)
    taps_store = pltpu.VMEM((taps, width), F32)

    queries, product = call(first_kernel, (wide, narrow), flops=6 * rows * width * width)(
        tokens, inv_rms_a[None], gain_a[None], proj_a
    )
    rim = lax.ppermute(product, "seq", [(i, i + 1) for i in range(devices - 1)])

    weights = mode_weights(rates_b, residues_b, float(devices * rows))
    near = call(near_kernel, wide, (own_store, taps_store), flops=8 * rows * rows * width)(
        product, taps_a
    )
    place = jnp.arange(rows, dtype=F32)[None, :, None]
    response = jnp.sum(weights[:, None] * jnp.exp(-rates_b[:, None] * place), 0)
    step = jnp.arange(SUB, dtype=F32)[None, :, None]
    rise = jnp.exp(-rates_b[:, None] * step)
    fall = jnp.exp(-rates_b[:, None] * (SUB - 1.0 - step))
    fade = jnp.exp(-rates_b * float(SUB))

    partial_a, signal, queries_b, state = call(
        middle_kernel,
        (narrow, wide, wide, jax.ShapeDtypeStruct((modes, width), F32)),
        (own_store, taps_store, pltpu.VMEM((rows, width), F32)),
        flops=8 * rows * rows * width,
    )(near, rim, taps_a, queries, out_a, tokens, inv_rms_b[None], gain_b[None], proj_b, fade, fall)

    before = states_before(state, rates_b, rows, devices)
    carry = before * (weights * jnp.exp(-rates_b))
    near_b = call(local_kernel, wide, (own_store,), flops=8 * rows * rows * width)(signal, response)
    partial_b = call(last_kernel, narrow, flops=4 * rows * width * width)(
        near_b, carry, rise, fade, queries_b, out_b
    )
    return (partial_a, partial_b)


def solution(mesh):
    placed = (
        P(("groups", "seq"), None),
        P(("groups", "seq")),
        P(),
        P(),
        P(),
        P(),
        P(("groups", "seq")),
        P(),
        P(),
        P(),
        P(),
        P(),
    )
    return jax.shard_map(
        on_device,
        mesh=mesh,
        in_specs=placed,
        out_specs=(P(("groups", "seq"), None), P(("groups", "seq"), None)),
        check_vma=False,
    )
```

time: 45 us -> 28.9 us (0.64)
  matrix products: 14 us -> 0 us
  blocking collectives: 9.48 us -> 0 us
  Pallas kernels: 0 us -> 5.11 us
  starting transfers between devices: 9.55 us -> 12.4 us
  other arithmetic: 1.02 us -> 0.57 us
    dot_general x22 -> x0, matrix products: 12 us -> none  [the longest x18 9.69 us: matmul(): return jnp.einsum(form, left, right, precision=HIGHEST_PREC)]
    ppermute x1 -> x7, starting transfers between devices: 2.36 us -> 12.4 us  [the longest x6 9.92 us: swap(): return lax.ppermute(block, 'seq', [(i, i ^ mask) for i in range(devices)])]
    all_to_all x1 -> x0, blocking collectives: 9.48 us -> none  [on_device(): lax.all_to_all(filtered, 'seq', split_axis=1, concat_axis=0, tiled=True)]
    all_to_all x1 -> x0, starting transfers between devices: 7.19 us -> none  [on_device(): lax.all_to_all(signal, 'seq', split_axis=0, concat_axis=1, tiled=True)]
    ppermute x1 -> x7, waiting for transfers between devices: 0.01 us -> 6.52 us  [the longest x6 6.52 us: swap(): return lax.ppermute(block, 'seq', [(i, i ^ mask) for i in range(devices)])]
    all_to_all x1 -> x0, waiting for transfers between devices: 6.28 us -> none  [on_device(): lax.all_to_all(signal, 'seq', split_axis=0, concat_axis=1, tiled=True)]
    pallas_call x0 -> x5, Pallas kernels: none -> 5.11 us  [the longest x1 1.89 us: on_device(): call(middle_kernel, (narrow, wide, wide, jax.ShapeDtypeStruct((modes, wid...]
    slice x1 -> x0, matrix products: 1.96 us -> none  [short_conv(): return result[0, 1:]]
  transfers between devices with their start and end apart: 2 -> 7, of which waited for: 1 -> 4; matrix products, arithmetic and copies ran while one was open for 10% -> 0% of each run, Pallas kernels for 0% -> 4%
where the time goes in v1:
time: 28.9 us; the launch traced here: 28.7 us
  starting transfers between devices  12.4 us (43%)
  waiting for transfers between devices  6.52 us (23%)
  Pallas kernels  5.11 us (18%)
  local copies, waits for them, and re-layouts  3.21 us (11%)
  between operations  0.83 us (3%)
  other arithmetic  0.57 us (2%)
    ppermute x6, starting transfers between devices, swap(): return lax.ppermute(block, 'seq', [(i, i ^ mask) for i in range(devices)])  9.92 us
    ppermute x6, waiting for transfers between devices, swap(): return lax.ppermute(block, 'seq', [(i, i ^ mask) for i in range(devices)])  6.52 us
    unnamed x26, local copies, waits for them, and re-layouts  3.21 us
    ppermute x1, starting transfers between devices, on_device(): rim = lax.ppermute(product, 'seq', [(i, i + 1) for i in range(devices - 1)])  2.49 us
    pallas_call x1, Pallas kernels, on_device(): call(middle_kernel, (narrow, wide, wide, jax.ShapeDtypeStruct((modes, wid...  1.89 us
    pallas_call x1, Pallas kernels, on_device(): call(local_kernel, wide, (own_store,), flops=8 * rows * rows * width)  1.02 us
    pallas_call x1, Pallas kernels, on_device(): call(near_kernel, wide, (own_store, taps_store), flops=8 * rows * rows *...  1.02 us
    pallas_call x1, Pallas kernels, on_device(): call(last_kernel, narrow, flops=4 * rows * width * width)  0.93 us
  transfers between devices with their start and end apart: 7, of which 4 were waited for; matrix products, arithmetic and copies ran while one was open for 0% of the time, Pallas kernels for 4%

profile of v1, /device:TPU:0, one launch (start us, length us, event | category | flops | bytes accessed | tf_op | source)
XLA Modules:
  0.0 28.7 jit_solution(17065550124690612572)
XLA Ops:
  0.6 1.0 %copy-done.1 = bf16[256,768]{1,0:T(8,128)(2,1)S(1)} copy-done((bf16[256,768]{1,0:T(8,128)(2,1)S(1)}, bf16[256,768]{1,0:T(8,128)(2,1)}, u32[]{:S(2)}) %copy-start.1) | copy-done | bytes 393240
  1.6 0.8 %copy-done.2 = bf16[128,256]{1,0:T(8,128)(2,1)S(1)} copy-done((bf16[128,256]{1,0:T(8,128)(2,1)S(1)}, bf16[128,256]{1,0:T(8,128)(2,1)}, u32[]{:S(2)}) %copy-start.2) | copy-done | bytes 65560
  2.5 0.7 %copy-done.7 = f32[256]{0:T(256)S(1)} copy-done((f32[256]{0:T(256)S(1)}, f32[256]{0:T(256)}, u32[]{:S(2)}) %copy-start.7) | copy-done | bytes 1048
  3.1 0.7 %copy-done.10 = f32[128]{0:T(128)S(1)} copy-done((f32[128]{0:T(128)S(1)}, f32[128]{0:T(128)}, u32[]{:S(2)}) %copy-start.10) | copy-done | bytes 536
  3.8 0.3 shard_map.131
  4.1 0.0 copy-start
  4.1 0.0 copy-start.3
  4.1 0.0 copy-start.5
  4.1 0.0 copy-start.8
  4.1 0.0 copy-start.9
  4.1 2.5 %collective-permute-start = (bf16[128,256]{1,0:T(8,128)(2,1)S(1)}, bf16[128,256]{1,0:T(8,128)(2,1)S(1)}, u32[]{:S(2)}, u32[]{:S(2)}) collective-permute-start(bf16[128,256]{1,0:T(8,128)(2,1)S(1)} %get-tuple-element.8.product), channel_id=1, source_target_pairs={{0,1},{1,2},{2,3},{3,4},{4,5},{5,6},{6,7},{7,8},{8,9},{9,10},{10,1... | collective-permute-start | bytes 196616 | tf_op jit(solution)/shard_map/ppermute | solution.py:219
  6.7 0.1 multiply_exponential_fusion
  6.8 1.0 %shard_map.132.near = f32[128,256]{1,0:T(8,128)S(1)} custom-call(bf16[128,256]{1,0:T(8,128)(2,1)S(1)} %get-tuple-element.8.product, bf16[128,256]{1,0:T(8,128)(2,1)S(1)} %copy-done.4), custom_call_target="tpu_custom_call" | custom-call | flops 33554432 | tf_op jit(solution)/shard_map/pallas_call | solution.py:222
  7.8 0.0 collective-permute-done.rim
  7.9 0.0 copy-start.12
  7.9 1.9 %shard_map.133 = (bf16[128,256]{1,0:T(8,128)(2,1)}, f32[128,256]{1,0:T(8,128)S(1)}, f32[128,256]{1,0:T(8,128)S(1)}, f32[16,256]{1,0:T(8,128)S(1)}) custom-call(f32[128,256]{1,0:T(8,128)S(1)} %shard_map.132.near, bf16[128,256]{1,0:T(8,128)(2,1)S(1)} %collective-permute-done.rim, bf16[128,256]{1,0:T(8,128)(2,1)S(1)} %copy-done.4, ...), custom_call_target="tpu_custom_call" | custom-call | flops 33554432 | tf_op jit(solution)/shard_map/pallas_call | solution.py:232
  9.8 3.9 %collective-permute-start.3 = (f32[16,256]{1,0:T(8,128)S(1)}, f32[16,256]{1,0:T(8,128)S(1)}, u32[]{:S(2)}, u32[]{:S(2)}) collective-permute-start(f32[16,256]{1,0:T(8,128)S(1)} %get-tuple-element.12), channel_id=1, source_target_pairs={{0,3},{1,2},{2,1},{3,0},{4,7},{5,6},{6,5},{7,4},{8,11},{9,10},{10,... | collective-permute-start | bytes 49160 | tf_op jit(solution)/shard_map/ppermute | solution.py:167
  13.6 1.1 %collective-permute-start.2 = (f32[16,256]{1,0:T(8,128)S(1)}, f32[16,256]{1,0:T(8,128)S(1)}, u32[]{:S(2)}, u32[]{:S(2)}) collective-permute-start(f32[16,256]{1,0:T(8,128)S(1)} %get-tuple-element.12), channel_id=1, source_target_pairs={{0,2},{1,3},{2,0},{3,1},{4,6},{5,7},{6,4},{7,5},{8,10},{9,11},{10,... | collective-permute-start | bytes 49160 | tf_op jit(solution)/shard_map/ppermute | solution.py:167
  14.7 0.1 collective-permute-start.1
  14.8 0.2 collective-permute-done.3
  15.1 2.3 %collective-permute-done.2 = f32[16,256]{1,0:T(8,128)S(1)} collective-permute-done((f32[16,256]{1,0:T(8,128)S(1)}, f32[16,256]{1,0:T(8,128)S(1)}, u32[]{:S(2)}, u32[]{:S(2)}) %collective-permute-start.2) | collective-permute-done | bytes 16416 | tf_op jit(solution)/shard_map/ppermute | solution.py:167
  17.4 0.0 collective-permute-done.1
  17.4 4.2 %collective-permute-start.6 = (f32[16,256]{1,0:T(8,128)S(1)}, f32[16,256]{1,0:T(8,128)S(1)}, u32[]{:S(2)}, u32[]{:S(2)}) collective-permute-start(f32[16,256]{1,0:T(8,128)S(1)} %multiply_add_fusion), channel_id=1, source_target_pairs={{0,12},{1,13},{2,14},{3,15},{4,8},{5,9},{6,10},{7,11},{8,4},{9,5},... | collective-permute-start | bytes 49160 | tf_op jit(solution)/shard_map/ppermute | solution.py:167
  21.6 0.0 collective-permute-start.5
  21.6 0.6 %collective-permute-start.4 = (f32[16,256]{1,0:T(8,128)S(1)}, f32[16,256]{1,0:T(8,128)S(1)}, u32[]{:S(2)}, u32[]{:S(2)}) collective-permute-start(f32[16,256]{1,0:T(8,128)S(1)} %multiply_add_fusion), channel_id=1, source_target_pairs={{0,4},{1,5},{2,6},{3,7},{4,0},{5,1},{6,2},{7,3},{8,12},{9,13},{10,... | collective-permute-start | bytes 49160 | tf_op jit(solution)/shard_map/ppermute | solution.py:167
  22.2 1.1 %collective-permute-done.6 = f32[16,256]{1,0:T(8,128)S(1)} collective-permute-done((f32[16,256]{1,0:T(8,128)S(1)}, f32[16,256]{1,0:T(8,128)S(1)}, u32[]{:S(2)}, u32[]{:S(2)}) %collective-permute-start.6) | collective-permute-done | bytes 16416 | tf_op jit(solution)/shard_map/ppermute | solution.py:167
  23.3 2.9 %collective-permute-done.5 = f32[16,256]{1,0:T(8,128)S(1)} collective-permute-done((f32[16,256]{1,0:T(8,128)S(1)}, f32[16,256]{1,0:T(8,128)S(1)}, u32[]{:S(2)}, u32[]{:S(2)}) %collective-permute-start.5) | collective-permute-done | bytes 16416 | tf_op jit(solution)/shard_map/ppermute | solution.py:167
  26.2 0.1 multiply_multiply_fusion
  26.3 0.4 %multiply_reduce_fusion.response = f32[128,256]{1,0:T(8,128)S(1)} fusion(f32[16,256]{1,0:T(8,128)S(1)} %get-tuple-element.18, f32[16,256]{1,0:T(8,128)S(1)} %get-tuple-element.15), kind=kLoop, calls=%fused_computation | loop fusion | flops 1540096 | bytes 163840 | tf_op jit(solution)/shard_map/reduce_sum | solution.py:226
  26.7 0.0 copy-start.6
  26.7 1.0 %shard_map.134.near = f32[128,256]{1,0:T(8,128)S(1)} custom-call(f32[128,256]{1,0:T(8,128)S(1)} %get-tuple-element.11.signal, f32[128,256]{1,0:T(8,128)S(1)} %multiply_reduce_fusion.response), custom_call_target="tpu_custom_call" | custom-call | flops 33554432 | tf_op jit(solution)/shard_map/pallas_call | solution.py:241
  27.7 0.9 %shard_map.135 = bf16[128,256]{1,0:T(8,128)(2,1)} custom-call(f32[128,256]{1,0:T(8,128)S(1)} %shard_map.134.near, f32[16,256]{1,0:T(8,128)S(1)} %get-tuple-element.14.carry, f32[16,8,256]{2,1,0:T(8,128)S(1)} %get-tuple-element.16.rise, f32[16,256]{1,0:T(8,128)S(1)} %get-tuple-element.19.fade, f32[128,256]{1,0:T(8,128)S(1)} %get-tuple-element.13.queries, ...), custom_call_target="tpu_custom_call" | custom-call | flops 33554432 | tf_op jit(solution)/shard_map/pallas_call | solution.py:242
  (19 shorter events, 0.1 us)
Async XLA Ops:
  0.6 1.0 %copy-start.1 = (bf16[256,768]{1,0:T(8,128)(2,1)S(1)}, bf16[256,768]{1,0:T(8,128)(2,1)}, u32[]{:S(2)}) copy-start(bf16[256,768]{1,0:T(8,128)(2,1)} %proj.2) | copy-start | bytes 1179652
  1.6 0.8 %copy-start.2 = (bf16[128,256]{1,0:T(8,128)(2,1)S(1)}, bf16[128,256]{1,0:T(8,128)(2,1)}, u32[]{:S(2)}) copy-start(bf16[128,256]{1,0:T(8,128)(2,1)} %tokens.3) | copy-start | bytes 196612
  2.5 0.7 %copy-start.7 = (f32[256]{0:T(256)S(1)}, f32[256]{0:T(256)}, u32[]{:S(2)}) copy-start(f32[256]{0:T(256)} %param.14) | copy-start | bytes 3076
  3.1 0.7 %copy-start.10 = (f32[128]{0:T(128)S(1)}, f32[128]{0:T(128)}, u32[]{:S(2)}) copy-start(f32[128]{0:T(128)} %param.13) | copy-start | bytes 1540
  3.8 2.8 %copy-start.11 = (f32[16,256]{1,0:T(8,128)S(1)}, f32[16,256]{1,0:T(8,128)}, u32[]{:S(2)}) copy-start(f32[16,256]{1,0:T(8,128)} %param.21) | copy-start | bytes 49156
  3.8 3.0 %copy-start.4 = (bf16[128,256]{1,0:T(8,128)(2,1)S(1)}, bf16[128,256]{1,0:T(8,128)(2,1)}, u32[]{:S(2)}) copy-start(bf16[128,256]{1,0:T(8,128)(2,1)} %taps.3) | copy-start | bytes 196612
  4.1 3.7 %copy-start = (bf16[256,768]{1,0:T(8,128)(2,1)S(1)}, bf16[256,768]{1,0:T(8,128)(2,1)}, u32[]{:S(2)}) copy-start(bf16[256,768]{1,0:T(8,128)(2,1)} %proj.3) | copy-start | bytes 1179652
  4.1 3.7 %copy-start.3 = (bf16[128,256]{1,0:T(8,128)(2,1)S(1)}, bf16[128,256]{1,0:T(8,128)(2,1)}, u32[]{:S(2)}) copy-start(bf16[128,256]{1,0:T(8,128)(2,1)} %tokens.3) | copy-start | bytes 196612
  4.1 3.7 %copy-start.5 = (bf16[256,256]{1,0:T(8,128)(2,1)S(1)}, bf16[256,256]{1,0:T(8,128)(2,1)}, u32[]{:S(2)}) copy-start(bf16[256,256]{1,0:T(8,128)(2,1)} %out_a.1) | copy-start | bytes 393220
  4.1 3.7 %copy-start.8 = (f32[256]{0:T(256)S(1)}, f32[256]{0:T(256)}, u32[]{:S(2)}) copy-start(f32[256]{0:T(256)} %param.19) | copy-start | bytes 3076
  4.1 3.7 %copy-start.9 = (f32[128]{0:T(128)S(1)}, f32[128]{0:T(128)}, u32[]{:S(2)}) copy-start(f32[128]{0:T(128)} %param.18) | copy-start | bytes 1540
  4.1 3.7 %collective-permute-start = (bf16[128,256]{1,0:T(8,128)(2,1)S(1)}, bf16[128,256]{1,0:T(8,128)(2,1)S(1)}, u32[]{:S(2)}, u32[]{:S(2)}) collective-permute-start(bf16[128,256]{1,0:T(8,128)(2,1)S(1)} %get-tuple-element.8.product), channel_id=1, source_target_pairs={{0,1},{1,2},{2,3},{3,4},{4,5},{5,6},{6,7},{7,8},{8,9},{9,10},{10,1... | collective-permute-start | bytes 196616 | tf_op jit(solution)/shard_map/ppermute | solution.py:219
  7.9 18.4 %copy-start.12 = (f32[16,256]{1,0:T(8,128)S(1)}, f32[16,256]{1,0:T(8,128)}, u32[]{:S(2)}) copy-start(f32[16,256]{1,0:T(8,128)} %param.22) | copy-start | bytes 49156
  9.8 5.3 %collective-permute-start.3 = (f32[16,256]{1,0:T(8,128)S(1)}, f32[16,256]{1,0:T(8,128)S(1)}, u32[]{:S(2)}, u32[]{:S(2)}) collective-permute-start(f32[16,256]{1,0:T(8,128)S(1)} %get-tuple-element.12), channel_id=1, source_target_pairs={{0,3},{1,2},{2,1},{3,0},{4,7},{5,6},{6,5},{7,4},{8,11},{9,10},{10,... | collective-permute-start | bytes 49160 | tf_op jit(solution)/shard_map/ppermute | solution.py:167
  13.6 3.7 %collective-permute-start.2 = (f32[16,256]{1,0:T(8,128)S(1)}, f32[16,256]{1,0:T(8,128)S(1)}, u32[]{:S(2)}, u32[]{:S(2)}) collective-permute-start(f32[16,256]{1,0:T(8,128)S(1)} %get-tuple-element.12), channel_id=1, source_target_pairs={{0,2},{1,3},{2,0},{3,1},{4,6},{5,7},{6,4},{7,5},{8,10},{9,11},{10,... | collective-permute-start | bytes 49160 | tf_op jit(solution)/shard_map/ppermute | solution.py:167
  14.7 2.6 %collective-permute-start.1 = (f32[16,256]{1,0:T(8,128)S(1)}, f32[16,256]{1,0:T(8,128)S(1)}, u32[]{:S(2)}, u32[]{:S(2)}) collective-permute-start(f32[16,256]{1,0:T(8,128)S(1)} %get-tuple-element.12), channel_id=1, source_target_pairs={{0,1},{1,0},{2,3},{3,2},{4,5},{5,4},{6,7},{7,6},{8,9},{9,8},{10,11... | collective-permute-start | bytes 49160 | tf_op jit(solution)/shard_map/ppermute | solution.py:167
  17.4 5.9 %collective-permute-start.6 = (f32[16,256]{1,0:T(8,128)S(1)}, f32[16,256]{1,0:T(8,128)S(1)}, u32[]{:S(2)}, u32[]{:S(2)}) collective-permute-start(f32[16,256]{1,0:T(8,128)S(1)} %multiply_add_fusion), channel_id=1, source_target_pairs={{0,12},{1,13},{2,14},{3,15},{4,8},{5,9},{6,10},{7,11},{8,4},{9,5},... | collective-permute-start | bytes 49160 | tf_op jit(solution)/shard_map/ppermute | solution.py:167
  21.6 4.6 %collective-permute-start.5 = (f32[16,256]{1,0:T(8,128)S(1)}, f32[16,256]{1,0:T(8,128)S(1)}, u32[]{:S(2)}, u32[]{:S(2)}) collective-permute-start(f32[16,256]{1,0:T(8,128)S(1)} %multiply_add_fusion), channel_id=1, source_target_pairs={{0,8},{1,9},{2,10},{3,11},{4,12},{5,13},{6,14},{7,15},{8,0},{9,1},... | collective-permute-start | bytes 49160 | tf_op jit(solution)/shard_map/ppermute | solution.py:167
  21.6 4.6 %collective-permute-start.4 = (f32[16,256]{1,0:T(8,128)S(1)}, f32[16,256]{1,0:T(8,128)S(1)}, u32[]{:S(2)}, u32[]{:S(2)}) collective-permute-start(f32[16,256]{1,0:T(8,128)S(1)} %multiply_add_fusion), channel_id=1, source_target_pairs={{0,4},{1,5},{2,6},{3,7},{4,0},{5,1},{6,2},{7,3},{8,12},{9,13},{10,... | collective-permute-start | bytes 49160 | tf_op jit(solution)/shard_map/ppermute | solution.py:167
  26.7 1.0 %copy-start.6 = (bf16[256,256]{1,0:T(8,128)(2,1)S(1)}, bf16[256,256]{1,0:T(8,128)(2,1)}, u32[]{:S(2)}) copy-start(bf16[256,256]{1,0:T(8,128)(2,1)} %out_b.1) | copy-start | bytes 393220

commit v2 on v1

v2 whole, which is shorter than its diff:
```python
import functools

import jax
import jax.numpy as jnp
from jax import lax
from jax.experimental import pallas as pl
from jax.experimental.pallas import tpu as pltpu
from jax.sharding import PartitionSpec as P

F32 = jnp.float32
BF16 = jnp.bfloat16
LANES = 128
SUB = 8
TAP_GROUP = 4
STEP = SUB * TAP_GROUP
VMEM_LIMIT = 32 * 1024 * 1024
WORK = 4 * 1024 * 1024


def call(kernel, outs, scratch, *arrays):
    spaces = [pltpu.HBM if isinstance(a, list) else pltpu.VMEM for a in arrays]
    placed = [
        pltpu.with_memory_space_constraint(a[0], pltpu.HBM) if isinstance(a, list) else a
        for a in arrays
    ]
    return pl.pallas_call(
        kernel,
        out_shape=outs,
        in_specs=[pl.BlockSpec(memory_space=space) for space in spaces],
        out_specs=[pl.BlockSpec(memory_space=out.memory_space) for out in outs],
        scratch_shapes=list(scratch),
        compiler_params=pltpu.CompilerParams(vmem_limit_bytes=VMEM_LIMIT),
        cost_estimate=pl.CostEstimate(flops=0, bytes_accessed=WORK, transcendentals=0),
    )(*placed)


def spread(scales, width):
    rows = scales.shape[1]
    square = jnp.transpose(jnp.broadcast_to(scales, (LANES, rows)))
    return jnp.concatenate([square] * (width // LANES), 1)


def scaled(values, scales, gain):
    return (values * spread(scales, values.shape[1]) * gain).astype(BF16)


def dot(left, right):
    return jnp.dot(left, right, preferred_element_type=F32)


def shifted_copies(values, store, lead):
    rows, width = values.shape
    tail = store.shape[1] - lead - rows
    if tail:
        values = jnp.concatenate([values, jnp.zeros((tail, width), F32)], 0)
    if lead:
        values = jnp.concatenate([jnp.zeros((lead, width), F32), values], 0)
    store[0] = values
    for r in range(1, SUB):
        store[r] = pltpu.roll(values, r, 0)


def tap_sum(taps, store, group, base, size):
    width = store.shape[2]

    def body(step, total):
        first = pl.multiple_of(base - step * SUB, SUB)
        for r in range(SUB):
            tap = taps[pl.ds((group * TAP_GROUP + step) * SUB + r, 1), :]
            total = total + tap * store[r, pl.ds(first, size), :]
        return total

    return lax.fori_loop(0, TAP_GROUP, body, jnp.zeros((size, width), F32))


def own_taps(values, taps, store, total):
    rows = values.shape[0]
    shifted_copies(values, store, STEP)
    total[...] = tap_sum(taps, store, 0, STEP, rows)
    for group in range(1, rows // STEP):
        skip = group * STEP
        total[pl.ds(skip, rows - skip), :] += tap_sum(taps, store, group, STEP, rows - skip)


def rim_taps(values, taps, store, total):
    rows = values.shape[0]
    shifted_copies(values, store, 0)
    for group in range(rows // STEP):
        size = (group + 1) * STEP
        total[pl.ds(0, size), :] += tap_sum(taps, store, group, rows - group * STEP, size)


def fetches(pairs, sems):
    copies = [pltpu.make_async_copy(a, b, sems.at[i]) for i, (a, b) in enumerate(pairs)]
    for copy in copies:
        copy.start()
    return copies


def first_kernel(
    tokens, inv_rms, gain, proj, taps, rates, residues, inv_rms_b, gain_b,
    product, normed, tokens_in, proj_q, taps_in, rates_in, residues_in, inv_rms_b_in, gain_b_in,
    proj_in, inv_rms_in, gain_in, sems,
):
    width = tokens.shape[1]
    copies = fetches(
        [
            (tokens, tokens_in),
            (inv_rms, inv_rms_in),
            (gain, gain_in),
            (proj.at[:, width:], proj_in),
            (proj.at[:, :width], proj_q),
            (taps, taps_in),
            (rates, rates_in),
            (residues, residues_in),
            (inv_rms_b, inv_rms_b_in),
            (gain_b, gain_b_in),
        ],
        sems,
    )
    for copy in copies[:3]:
        copy.wait()
    normed[...] = scaled(tokens_in[...].astype(F32), inv_rms_in[...], gain_in[...])
    copies[3].wait()
    pair = dot(normed[...], proj_in[...])
    product[...] = (pair[:, :width] * pair[:, width:]).astype(BF16)
    for copy in copies[4:]:
        copy.wait()


def near_kernel(
    devices, product, normed, proj_q, taps, rates, residues, inv_rms, gain, out_a, out_b, proj,
    total, queries, taps_wide, scale, weights, rise, fall, fade, shares, out_a_in, out_b_in, proj_in,
    store, sems,
):
    copies = fetches([(out_a, out_a_in), (proj, proj_in), (out_b, out_b_in)], sems)
    rows, width = product.shape
    modes = rates.shape[0]
    taps_wide[...] = taps[...].astype(F32)
    own_taps(product[...].astype(F32), taps_wide, store, total)
    queries[...] = dot(normed[...], proj_q[...])
    scale[...] = spread(inv_rms[...], width) * gain[...]
    rate = rates[...]
    weight = mode_weights(rate, residues[...], float(devices * rows))
    weights[...] = weight
    fade[...] = jnp.exp(rate * -float(SUB))
    step = lax.broadcasted_iota(jnp.int32, (SUB, width), 0).astype(F32)
    for m in range(modes):
        rise[m] = jnp.exp(-rate[m : m + 1] * step)
        fall[m] = jnp.exp(-rate[m : m + 1] * (SUB - 1.0 - step))
    me = lax.axis_index("seq")
    weight = weight * jnp.exp(-rate)
    for i, (last, count, keep) in enumerate(share_plan(me, devices, rows)):
        share = jnp.exp(-rate * jnp.maximum(count, 0).astype(F32))
        if last:
            share = jnp.where(keep, share * weight, 0.0)
        shares[i] = share
    for copy in copies:
        copy.wait()


def middle_kernel(
    near, rim_chain, rim_pair, taps, queries, out_a, tokens, scale, proj, fade, fall,
    partial, signal, normed_b, state, store, total,
):
    width = near.shape[1]
    modes = fade.shape[0]
    me = lax.axis_index("seq")
    total[...] = near[...]
    rim = jnp.where(me % 2 == 1, rim_pair[...].astype(F32), rim_chain[...].astype(F32))
    rim_taps(jnp.where(me == 0, 0.0, rim), taps, store, total)
    gated = (queries[...] * total[...]).astype(BF16)
    term = dot(gated, out_a[...]).astype(BF16)
    partial[...] = term
    hidden = (tokens[...].astype(F32) + term.astype(F32)).astype(BF16)
    normed = (hidden.astype(F32) * scale[...]).astype(BF16)
    normed_b[...] = normed
    pair = dot(normed, proj[:, width:])
    mixed = (pair[:, :width] * pair[:, width:]).astype(BF16).astype(F32)
    signal[...] = mixed
    for lane in range(0, width, LANES):
        here = slice(lane, lane + LANES)
        for m in range(modes):
            drop = fade[m : m + 1, here]
            held = mixed[:SUB, here]
            for row in range(SUB, mixed.shape[0], SUB):
                held = held * drop + mixed[row : row + SUB, here]
            state[m : m + 1, here] = jnp.sum(held * fall[m, :, here], 0, keepdims=True)


def local_kernel(
    signal, weights, rise, fade, normed, proj, partial,
    total, queries, partial_out, response, store, sems,
):
    copies = fetches([(partial, partial_out)], sems)
    rows, width = signal.shape
    modes = fade.shape[0]
    for lane in range(0, width, LANES):
        here = slice(lane, lane + LANES)
        sums = [jnp.zeros((SUB, LANES), F32)] * (rows // SUB)
        for m in range(modes):
            add_fading(sums, weights[m : m + 1, here] * rise[m, :, here], fade[m : m + 1, here])
        for i, part in enumerate(sums):
            response[i * SUB : (i + 1) * SUB, here] = part
    own_taps(signal[...], response, store, total)
    queries[...] = dot(normed[...], proj[:, :width])
    for copy in copies:
        copy.wait()


def add_fading(sums, held, drop):
    for i in range(len(sums)):
        sums[i] = sums[i] + held
        if i + 1 < len(sums):
            held = held * drop


def last_kernel(near, carry, rise, fade, queries, out_b, partial, held, sems):
    rows, width = near.shape
    modes = fade.shape[0]
    columns = []
    for lane in range(0, width, LANES):
        here = slice(lane, lane + LANES)
        sums = [near[row : row + SUB, here] for row in range(0, rows, SUB)]
        for m in range(modes):
            add_fading(sums, carry[m : m + 1, here] * rise[m, :, here], fade[m : m + 1, here])
        columns.append(jnp.concatenate(sums, 0))
    long_out = jnp.concatenate(columns, 1).astype(BF16).astype(F32)
    gated = (queries[...] * long_out).astype(BF16)
    held[...] = dot(gated, out_b[...]).astype(BF16)
    for copy in fetches([(held, partial)], sems):
        copy.wait()


def mode_weights(rates, residues, length):
    energy = one_less_exp(2.0 * rates) / one_less_exp(2.0 * rates * length)
    return residues * jnp.sqrt(energy)


def one_less_exp(value):
    series = jnp.ones_like(value)
    for n in range(9, 1, -1):
        series = 1.0 - value * (1.0 / n) * series
    return jnp.where(value < 0.25, value * series, 1.0 - jnp.exp(-value))


def levels(devices):
    found, stride = [], 1
    while stride < devices:
        radix = 4 if devices // stride % 4 == 0 else 2
        found.append((stride, radix))
        stride *= radix
    assert stride == devices
    return found


def share_plan(me, devices, rows):
    plan = []
    for stride, radix in levels(devices):
        place = me // stride % radix
        for k in range(1, radix):
            other = place ^ k
            gap = ((place - 1 - other) * stride + me % stride) * rows
            plan.append((True, gap, other < place))
        if stride * radix < devices:
            for k in range(radix):
                plan.append((False, (radix - 1 - (place ^ k)) * stride * rows, None))
    return plan


def swap(block, devices, mask):
    return lax.ppermute(block, "seq", [(i, i ^ mask) for i in range(devices)])


def chain(block, devices):
    route = [(i, i + 1) for i in range(1, devices - 1, 2)]
    if devices < 8:
        free = [*range(0, devices, 2), devices - 1]
        route += list(zip(free, [0, *range(1, devices, 2)]))
    else:
        route += [(i, i - 1) for i in range(4, devices - 2, 2)]
        route += [(0, 1), (2, 0), (devices - 2, devices - 1), (devices - 1, devices - 3)]
    return lax.ppermute(block, "seq", route)


def carry_in(state, shares, near, devices):
    before, total, at = 0.0, state, 0
    for stride, radix in levels(devices):
        cross = 1 if stride > 1 else 0
        parts = [total]
        for k in range(radix - 1, 0, -1):
            parts.insert(1, swap(total, devices, k * stride + cross * (k % 2)))
        for k in range(radix - 1, 0, -1):
            before = before + parts[k] * shares[at + k - 1]
        at += radix - 1
        if stride * radix < devices:
            total = sum(parts[k] * shares[at + k] for k in range(radix - 1, -1, -1))
            at += radix
        if stride == 1:
            total, near = lax.optimization_barrier((total, near))
    return before, near


def on_device(
    tokens,
    inv_rms_a,
    gain_a,
    proj_a,
    taps_a,
    out_a,
    inv_rms_b,
    gain_b,
    proj_b,
    rates_b,
    residues_b,
    out_b,
):
    rows, width = tokens.shape
    taps = taps_a.shape[0]
    modes = rates_b.shape[0]
    devices = lax.axis_size("seq")
    assert taps == rows and rows % STEP == 0 and devices > 2
    wide = pltpu.VMEM((rows, width), F32)
    narrow = pltpu.VMEM((rows, width), BF16)
    square = pltpu.VMEM((width, width), BF16)
    bank = pltpu.VMEM((modes, SUB, width), F32)
    states = pltpu.VMEM((modes, width), F32)
    by_token = pltpu.VMEM((1, rows), F32)
    by_channel = pltpu.VMEM((1, width), F32)
    store = pltpu.VMEM((SUB, rows + STEP, width), F32)
    semaphores = pltpu.SemaphoreType.DMA

    product, normed, tokens, proj_q, taps_a, rates, residues, inv_rms, gain = call(
        first_kernel,
        (narrow, narrow, narrow, square, narrow, states, states, by_token, by_channel),
        (pltpu.VMEM((width, 2 * width), BF16), by_token, by_channel, semaphores((10,))),
        [tokens], [inv_rms_a[None]], [gain_a[None]], [proj_a], [taps_a], [rates_b], [residues_b],
        [inv_rms_b[None]], [gain_b[None]],
    )
    rim_chain = chain(product, devices)
    rim_pair = swap(product, devices, 1)

    shares = pltpu.VMEM((len(share_plan(0, devices, rows)), modes, width), F32)
    (
        near, queries, taps_wide, scale, weights, rise, fall, fade, shares, out_a, out_b, proj_b,
    ) = call(
        functools.partial(near_kernel, devices),
        (
            wide, wide, wide, wide, states, bank, bank, states, shares,
            square, square, pltpu.VMEM(proj_b.shape, BF16),
        ),
        (store, semaphores((3,))),
        product, normed, proj_q, taps_a, rates, residues, inv_rms, gain, [out_a], [out_b], [proj_b],
    )

    partial_a, signal, normed_b, state = call(
        middle_kernel, (narrow, wide, narrow, states), (store, wide),
        near, rim_chain, rim_pair, taps_wide, queries, out_a, tokens, scale, proj_b, fade, fall,
    )
    near_b, queries_b, partial_a = call(
        local_kernel,
        (wide, wide, pltpu.HBM((rows, width), BF16)),
        (wide, store, semaphores((1,))),
        signal, weights, rise, fade, normed_b, proj_b, partial_a,
    )
    carry, near_b = carry_in(state, shares, near_b, devices)
    (partial_b,) = call(
        last_kernel, (pltpu.HBM((rows, width), BF16),), (narrow, semaphores((1,))),
        near_b, carry, rise, fade, queries_b, out_b,
    )
    return (partial_a, partial_b)


def solution(mesh):
    placed = (
        P(("groups", "seq"), None),
        P(("groups", "seq")),
        P(),
        P(),
        P(),
        P(),
        P(("groups", "seq")),
        P(),
        P(),
        P(),
        P(),
        P(),
    )
    return jax.shard_map(
        on_device,
        mesh=mesh,
        in_specs=placed,
        out_specs=(P(("groups", "seq"), None), P(("groups", "seq"), None)),
        check_vma=False,
    )
```

time: 28.9 us -> 22.2 us (0.77)
  starting transfers between devices: 12.4 us -> 9.04 us
  local copies, waits for them, and re-layouts: 3.21 us -> 0 us
  Pallas kernels: 5.11 us -> 6.33 us
  other arithmetic: 0.57 us -> 0.03 us
  waiting for transfers between devices: 6.52 us -> 6 us
    unnamed x26 -> x0, local copies, waits for them, and re-layouts: 3.21 us -> none
    ppermute x1, starting transfers between devices: 2.49 us -> 0.51 us  [chain(): return lax.ppermute(block, 'seq', route)]
    ppermute x6 -> x7, waiting for transfers between devices: 6.52 us -> 5.12 us  [swap(): return lax.ppermute(block, 'seq', [(i, i ^ mask) for i in range(devices)])]
    ppermute x6 -> x7, starting transfers between devices: 9.92 us -> 8.53 us  [swap(): return lax.ppermute(block, 'seq', [(i, i ^ mask) for i in range(devices)])]
    pallas_call x5, Pallas kernels: 5.11 us -> 6.33 us  [call(): pl.pallas_call(kernel, out_shape=outs, in_specs=[pl.BlockSpec(memory_spac...]
    ppermute x1, waiting for transfers between devices: 0.01 us -> 0.88 us  [chain(): return lax.ppermute(block, 'seq', route)]
    reduce_sum x1 -> x0, other arithmetic: 0.37 us -> none  [on_device(): response = jnp.sum(weights[:, None] * jnp.exp(-rates_b[:, None] * place), 0)]
  transfers between devices with their start and end apart: 7 -> 8, of which waited for: 4 -> 4; matrix products, arithmetic and copies ran while one was open for 0% -> 0% of each run, Pallas kernels for 4% -> 12%
where the time goes in v2:
time: 22.2 us; the launch traced here: 22.1 us
  starting transfers between devices  9.04 us (41%)
  Pallas kernels  6.33 us (29%)
  waiting for transfers between devices  6 us (27%)
  between operations  0.68 us (3%)
    ppermute x7, starting transfers between devices, swap(): return lax.ppermute(block, 'seq', [(i, i ^ mask) for i in range(devices)])  8.53 us
    pallas_call x5, Pallas kernels, call(): pl.pallas_call(kernel, out_shape=outs, in_specs=[pl.BlockSpec(memory_spac...  6.33 us
    ppermute x7, waiting for transfers between devices, swap(): return lax.ppermute(block, 'seq', [(i, i ^ mask) for i in range(devices)])  5.12 us
    ppermute x1, waiting for transfers between devices, chain(): return lax.ppermute(block, 'seq', route)  0.88 us
    ppermute x1, starting transfers between devices, chain(): return lax.ppermute(block, 'seq', route)  0.51 us
  transfers between devices with their start and end apart: 8, of which 4 were waited for; matrix products, arithmetic and copies ran while one was open for 0% of the time, Pallas kernels for 12%

profile of v2, /device:TPU:0, one launch (start us, length us, event | category | flops | bytes accessed | tf_op | source)
XLA Modules:
  0.0 22.1 jit_solution(5784860048773634182)
XLA Ops:
  0.6 1.3 %shard_map.131 = (bf16[128,256]{1,0:T(8,128)(2,1)S(1)}, bf16[128,256]{1,0:T(8,128)(2,1)S(1)}, bf16[128,256]{1,0:T(8,128)(2,1)S(1)}, bf16[256,256]{1,0:T(8,128)(2...) custom-call(bf16[128,256]{1,0:T(8,128)(2,1)} %tokens.1, ...), custom_call_target="tpu_custom_call" | custom-call | bytes 4194304 | tf_op jit(solution)/shard_map/pallas_call | solution.py:26
  2.0 0.5 %collective-permute-start = (bf16[128,256]{1,0:T(8,128)(2,1)S(1)}, bf16[128,256]{1,0:T(8,128)(2,1)S(1)}, u32[]{:S(2)}, u32[]{:S(2)}) collective-permute-start(bf16[128,256]{1,0:T(8,128)(2,1)S(1)} %get-tuple-element.32.product), channel_id=1, source_target_pairs={{1,2},{3,4},{5,6},{7,8},{9,10},{11,12},{13,14},{4,3},{6,5},{8,7},{... | collective-permute-start | bytes 196616 | tf_op jit(solution)/shard_map/ppermute | solution.py:283
  2.5 2.6 %collective-permute-start.1 = (bf16[128,256]{1,0:T(8,128)(2,1)S(1)}, bf16[128,256]{1,0:T(8,128)(2,1)S(1)}, u32[]{:S(2)}, u32[]{:S(2)}) collective-permute-start(bf16[128,256]{1,0:T(8,128)(2,1)S(1)} %get-tuple-element.32.product), channel_id=1, source_target_pairs={{0,1},{1,0},{2,3},{3,2},{4,5},{5,4},{6,7},{7,6},{8,9},{9,8},{10,11... | collective-permute-start | bytes 196616 | tf_op jit(solution)/shard_map/ppermute | solution.py:272
  5.1 1.2 %shard_map.132 = (f32[128,256]{1,0:T(8,128)S(1)}, f32[128,256]{1,0:T(8,128)S(1)}, f32[128,256]{1,0:T(8,128)S(1)}, f32[128,256]{1,0:T(8,128)S(1)}, f32[16,256]{1,...) custom-call(bf16[128,256]{1,0:T(8,128)(2,1)S(1)} %get-tuple-element., ...), custom_call_target="tpu_custom_call" | custom-call | bytes 4194304 | tf_op jit(solution)/shard_map/pallas_call | solution.py:26
  6.3 0.9 %collective-permute-done.rim_chain = bf16[128,256]{1,0:T(8,128)(2,1)S(1)} collective-permute-done((bf16[128,256]{1,0:T(8,128)(2,1)S(1)}, bf16[128,256]{1,0:T(8,128)(2,1)S(1)}, u32[]{:S(2)}, u32[]{:S(2)}) %collective-permute-start) | collective-permute-done | bytes 65568 | tf_op jit(solution)/shard_map/ppermute | solution.py:283
  7.2 0.0 collective-permute-done.1.rim_pair
  7.2 1.5 %shard_map.133 = (bf16[128,256]{1,0:T(8,128)(2,1)S(1)}, f32[128,256]{1,0:T(8,128)S(1)}, bf16[128,256]{1,0:T(8,128)(2,1)S(1)}, f32[16,256]{1,0:T(8,128)S(1)}) custom-call(f32[128,256]{1,0:T(8,128)S(1)} %get-tuple-element.40.near, bf16[128,256]{1,0:T(8,128)(2,1)S(1)} %collective-permute-done.rim_chain, bf16[128,256]{1,0:T(8,128)(2,1)S(1)} %collective-permute-done.1.rim_pair, ...), custom_call_target="tpu_custom_call" | custom-call | bytes 4194304 | tf_op jit(solution)/shard_map/pallas_call | solution.py:26
  8.7 1.8 %collective-permute-start.2 = (f32[16,256]{1,0:T(8,128)S(1)}, f32[16,256]{1,0:T(8,128)S(1)}, u32[]{:S(2)}, u32[]{:S(2)}) collective-permute-start(f32[16,256]{1,0:T(8,128)S(1)} %get-tuple-element.55), channel_id=1, source_target_pairs={{0,3},{1,2},{2,1},{3,0},{4,7},{5,6},{6,5},{7,4},{8,11},{9,10},{10,... | collective-permute-start | bytes 49160 | tf_op jit(solution)/shard_map/ppermute | solution.py:272
  10.6 0.0 collective-permute-start.3
  10.6 0.2 collective-permute-start.4
  10.8 1.3 %shard_map.134 = (f32[128,256]{1,0:T(8,128)S(1)}, f32[128,256]{1,0:T(8,128)S(1)}, bf16[128,256]{1,0:T(8,128)(2,1)}) custom-call(f32[128,256]{1,0:T(8,128)S(1)} %get-tuple-element.49.signal, f32[16,256]{1,0:T(8,128)S(1)} %get-tuple-element.50.weights, f32[16,8,256]{2,1,0:T(8,128)S(1)} %get-tuple-element.51.rise, f32[16,256]{1,0:T(8,128)S(1)} %get-tuple-element.47.fade, ...), custom_call_target="tpu_custom_call" | custom-call | bytes 4194304 | tf_op jit(solution)/shard_map/pallas_call | solution.py:26
  12.1 0.0 collective-permute-done.2
  12.1 2.2 %collective-permute-done.3 = f32[16,256]{1,0:T(8,128)S(1)} collective-permute-done((f32[16,256]{1,0:T(8,128)S(1)}, f32[16,256]{1,0:T(8,128)S(1)}, u32[]{:S(2)}, u32[]{:S(2)}) %collective-permute-start.3) | collective-permute-done | bytes 16416 | tf_op jit(solution)/shard_map/ppermute | solution.py:272
  14.3 0.0 collective-permute-done.4
  14.3 1.9 %collective-permute-start.5 = (f32[16,256]{1,0:T(8,128)S(1)}, f32[16,256]{1,0:T(8,128)S(1)}, u32[]{:S(2)}, u32[]{:S(2)}) collective-permute-start(f32[16,256]{1,0:T(8,128)S(1)} %fusion.5), channel_id=1, source_target_pairs={{0,13},{1,12},{2,15},{3,14},{4,9},{5,8},{6,11},{7,10},{8,5},{9,4},... | collective-permute-start | bytes 49160 | tf_op jit(solution)/shard_map/ppermute | solution.py:272
  16.2 0.8 %collective-permute-start.6 = (f32[16,256]{1,0:T(8,128)S(1)}, f32[16,256]{1,0:T(8,128)S(1)}, u32[]{:S(2)}, u32[]{:S(2)}) collective-permute-start(f32[16,256]{1,0:T(8,128)S(1)} %fusion.5), channel_id=1, source_target_pairs={{0,8},{1,9},{2,10},{3,11},{4,12},{5,13},{6,14},{7,15},{8,0},{9,1},... | collective-permute-start | bytes 49160 | tf_op jit(solution)/shard_map/ppermute | solution.py:272
  17.1 1.2 %collective-permute-start.7 = (f32[16,256]{1,0:T(8,128)S(1)}, f32[16,256]{1,0:T(8,128)S(1)}, u32[]{:S(2)}, u32[]{:S(2)}) collective-permute-start(f32[16,256]{1,0:T(8,128)S(1)} %fusion.5), channel_id=1, source_target_pairs={{0,5},{1,4},{2,7},{3,6},{4,1},{5,0},{6,3},{7,2},{8,13},{9,12},{10,... | collective-permute-start | bytes 49160 | tf_op jit(solution)/shard_map/ppermute | solution.py:272
  18.2 1.1 %collective-permute-done.5 = f32[16,256]{1,0:T(8,128)S(1)} collective-permute-done((f32[16,256]{1,0:T(8,128)S(1)}, f32[16,256]{1,0:T(8,128)S(1)}, u32[]{:S(2)}, u32[]{:S(2)}) %collective-permute-start.5) | collective-permute-done | bytes 16416 | tf_op jit(solution)/shard_map/ppermute | solution.py:272
  19.4 1.8 %collective-permute-done.6 = f32[16,256]{1,0:T(8,128)S(1)} collective-permute-done((f32[16,256]{1,0:T(8,128)S(1)}, f32[16,256]{1,0:T(8,128)S(1)}, u32[]{:S(2)}, u32[]{:S(2)}) %collective-permute-start.6) | collective-permute-done | bytes 16416 | tf_op jit(solution)/shard_map/ppermute | solution.py:272
  21.1 0.0 collective-permute-done.7
  21.1 0.9 %shard_map.135 = bf16[128,256]{1,0:T(8,128)(2,1)} custom-call(f32[128,256]{1,0:T(8,128)S(1)} %get-tuple-element.58.near, f32[16,256]{1,0:T(8,128)S(1)} %fusion.carry, f32[16,8,256]{2,1,0:T(8,128)S(1)} %get-tuple-element.51.rise, f32[16,256]{1,0:T(8,128)S(1)} %get-tuple-element.47.fade, f32[128,256]{1,0:T(8,128)S(1)} %get-tuple-element.60.queries, ...), custom_call_target="tpu_custom_call" | custom-call | bytes 4194304 | tf_op jit(solution)/shard_map/pallas_call | solution.py:26
  (2 shorter events, 0.0 us)
Async XLA Ops:
  2.0 5.2 %collective-permute-start = (bf16[128,256]{1,0:T(8,128)(2,1)S(1)}, bf16[128,256]{1,0:T(8,128)(2,1)S(1)}, u32[]{:S(2)}, u32[]{:S(2)}) collective-permute-start(bf16[128,256]{1,0:T(8,128)(2,1)S(1)} %get-tuple-element.32.product), channel_id=1, source_target_pairs={{1,2},{3,4},{5,6},{7,8},{9,10},{11,12},{13,14},{4,3},{6,5},{8,7},{... | collective-permute-start | bytes 196616 | tf_op jit(solution)/shard_map/ppermute | solution.py:283
  2.5 4.7 %collective-permute-start.1 = (bf16[128,256]{1,0:T(8,128)(2,1)S(1)}, bf16[128,256]{1,0:T(8,128)(2,1)S(1)}, u32[]{:S(2)}, u32[]{:S(2)}) collective-permute-start(bf16[128,256]{1,0:T(8,128)(2,1)S(1)} %get-tuple-element.32.product), channel_id=1, source_target_pairs={{0,1},{1,0},{2,3},{3,2},{4,5},{5,4},{6,7},{7,6},{8,9},{9,8},{10,11... | collective-permute-start | bytes 196616 | tf_op jit(solution)/shard_map/ppermute | solution.py:272
  8.7 3.4 %collective-permute-start.2 = (f32[16,256]{1,0:T(8,128)S(1)}, f32[16,256]{1,0:T(8,128)S(1)}, u32[]{:S(2)}, u32[]{:S(2)}) collective-permute-start(f32[16,256]{1,0:T(8,128)S(1)} %get-tuple-element.55), channel_id=1, source_target_pairs={{0,3},{1,2},{2,1},{3,0},{4,7},{5,6},{6,5},{7,4},{8,11},{9,10},{10,... | collective-permute-start | bytes 49160 | tf_op jit(solution)/shard_map/ppermute | solution.py:272
  10.6 3.7 %collective-permute-start.3 = (f32[16,256]{1,0:T(8,128)S(1)}, f32[16,256]{1,0:T(8,128)S(1)}, u32[]{:S(2)}, u32[]{:S(2)}) collective-permute-start(f32[16,256]{1,0:T(8,128)S(1)} %get-tuple-element.55), channel_id=1, source_target_pairs={{0,2},{1,3},{2,0},{3,1},{4,6},{5,7},{6,4},{7,5},{8,10},{9,11},{10,... | collective-permute-start | bytes 49160 | tf_op jit(solution)/shard_map/ppermute | solution.py:272
  10.6 3.7 %collective-permute-start.4 = (f32[16,256]{1,0:T(8,128)S(1)}, f32[16,256]{1,0:T(8,128)S(1)}, u32[]{:S(2)}, u32[]{:S(2)}) collective-permute-start(f32[16,256]{1,0:T(8,128)S(1)} %get-tuple-element.55), channel_id=1, source_target_pairs={{0,1},{1,0},{2,3},{3,2},{4,5},{5,4},{6,7},{7,6},{8,9},{9,8},{10,11... | collective-permute-start | bytes 49160 | tf_op jit(solution)/shard_map/ppermute | solution.py:272
  14.3 5.0 %collective-permute-start.5 = (f32[16,256]{1,0:T(8,128)S(1)}, f32[16,256]{1,0:T(8,128)S(1)}, u32[]{:S(2)}, u32[]{:S(2)}) collective-permute-start(f32[16,256]{1,0:T(8,128)S(1)} %fusion.5), channel_id=1, source_target_pairs={{0,13},{1,12},{2,15},{3,14},{4,9},{5,8},{6,11},{7,10},{8,5},{9,4},... | collective-permute-start | bytes 49160 | tf_op jit(solution)/shard_map/ppermute | solution.py:272
  16.2 4.9 %collective-permute-start.6 = (f32[16,256]{1,0:T(8,128)S(1)}, f32[16,256]{1,0:T(8,128)S(1)}, u32[]{:S(2)}, u32[]{:S(2)}) collective-permute-start(f32[16,256]{1,0:T(8,128)S(1)} %fusion.5), channel_id=1, source_target_pairs={{0,8},{1,9},{2,10},{3,11},{4,12},{5,13},{6,14},{7,15},{8,0},{9,1},... | collective-permute-start | bytes 49160 | tf_op jit(solution)/shard_map/ppermute | solution.py:272
  17.1 4.1 %collective-permute-start.7 = (f32[16,256]{1,0:T(8,128)S(1)}, f32[16,256]{1,0:T(8,128)S(1)}, u32[]{:S(2)}, u32[]{:S(2)}) collective-permute-start(f32[16,256]{1,0:T(8,128)S(1)} %fusion.5), channel_id=1, source_target_pairs={{0,5},{1,4},{2,7},{3,6},{4,1},{5,0},{6,3},{7,2},{8,13},{9,12},{10,... | collective-permute-start | bytes 49160 | tf_op jit(solution)/shard_map/ppermute | solution.py:272

commit v3 on v2

--- a/solution.py
+++ b/solution.py
@@ -150,11 +150,9 @@
         fall[m] = jnp.exp(-rate[m : m + 1] * (SUB - 1.0 - step))
     me = lax.axis_index("seq")
     weight = weight * jnp.exp(-rate)
-    for i, (last, count, keep) in enumerate(share_plan(me, devices, rows)):
+    for i, (weighted, count, keep) in enumerate(share_plan(me, devices, rows)):
         share = jnp.exp(-rate * jnp.maximum(count, 0).astype(F32))
-        if last:
-            share = jnp.where(keep, share * weight, 0.0)
-        shares[i] = share
+        shares[i] = jnp.where(keep, share * weight if weighted else share, 0.0)
     for copy in copies:
         copy.wait()
 
@@ -245,27 +243,37 @@
 
 
 def levels(devices):
-    found, stride = [], 1
+    found, stride = [], 2
     while stride < devices:
-        radix = 4 if devices // stride % 4 == 0 else 2
+        radix = max(r for r in (2, 4, 8) if devices // stride % r == 0)
         found.append((stride, radix))
         stride *= radix
     assert stride == devices
     return found
 
 
+def routes(radix):
+    return [(k + 1, k) for k in range(radix - 2, 0, -2)] + [(1, 1)]
+
+
 def share_plan(me, devices, rows):
-    plan = []
+    core = me % 2
+    yes = me >= 0
+    plan = [(False, (1 - core) * rows, yes), (False, core * rows, yes)]
     for stride, radix in levels(devices):
         place = me // stride % radix
-        for k in range(1, radix):
-            other = place ^ k
-            gap = ((place - 1 - other) * stride + me % stride) * rows
-            plan.append((True, gap, other < place))
-        if stride * radix < devices:
-            for k in range(radix):
-                plan.append((False, (radix - 1 - (place ^ k)) * stride * rows, None))
-    return plan
+        inner = me % stride // 2 * 2
+        last = stride * radix == devices
+        for even, odd in routes(radix):
+            other = place ^ jnp.where(core == 0, odd, even)
+            once = (core == 0) if even == odd else yes
+            gap = ((place - 1 - other) * stride + inner) * rows
+            plan.append((False, gap, (other < place) & once))
+            if not last:
+                plan.append((False, (radix - 1 - other) * stride * rows, once))
+        if not last:
+            plan.append((False, (radix - 1 - place) * stride * rows, core == 0))
+    return plan + [(True, core * rows, yes), (True, 0 * core, core == 1)]
 
 
 def swap(block, devices, mask):
@@ -283,22 +291,32 @@
     return lax.ppermute(block, "seq", route)
 
 
+def cross(block, devices, stride, even, odd):
+    masks = (even * stride + 1, odd * stride + 1)
+    return lax.ppermute(block, "seq", [(i, i ^ masks[i % 2]) for i in range(devices)])
+
+
 def carry_in(state, shares, near, devices):
-    before, total, at = 0.0, state, 0
+    share = iter([shares[i] for i in range(shares.shape[0])])
+    beside = swap(state, devices, 1)
+    total = state * next(share) + beside * next(share)
+    before = None
     for stride, radix in levels(devices):
-        cross = 1 if stride > 1 else 0
-        parts = [total]
-        for k in range(radix - 1, 0, -1):
-            parts.insert(1, swap(total, devices, k * stride + cross * (k % 2)))
-        for k in range(radix - 1, 0, -1):
-            before = before + parts[k] * shares[at + k - 1]
-        at += radix - 1
-        if stride * radix < devices:
-            total = sum(parts[k] * shares[at + k] for k in range(radix - 1, -1, -1))
-            at += radix
-        if stride == 1:
-            total, near = lax.optimization_barrier((total, near))
-    return before, near
+        parts = [cross(total, devices, stride, even, odd) for even, odd in routes(radix)]
+        last = stride * radix == devices
+        sums, totals = [], []
+        for part in parts:
+            sums.append(part * next(share))
+            if not last:
+                totals.append(part * next(share))
+        half = functools.reduce(jnp.add, sums)
+        before = half if before is None else before + half
+        if not last:
+            half = functools.reduce(jnp.add, totals) + total * next(share)
+            total = half + swap(half, devices, 1)
+    before, near = lax.optimization_barrier((before, near))
+    before = before + swap(before, devices, 1)
+    return before * next(share) + beside * next(share), near
 
 
 def on_device(

time: 22.2 us -> 21.6 us (0.973)
  waiting for transfers between devices: 6 us -> 3.93 us
  starting transfers between devices: 9.04 us -> 10.5 us
    ppermute x0 -> x4, starting transfers between devices: none -> 6.03 us  [cross(): lax.ppermute(block, 'seq', [(i, i ^ masks[i % 2]) for i in range(devices)])]
    ppermute x7 -> x3, starting transfers between devices: 8.53 us -> 3.92 us  [swap(): return lax.ppermute(block, 'seq', [(i, i ^ mask) for i in range(devices)])]
    ppermute x7 -> x3, waiting for transfers between devices: 5.12 us -> 2.01 us  [swap(): return lax.ppermute(block, 'seq', [(i, i ^ mask) for i in range(devices)])]
    ppermute x0 -> x4, waiting for transfers between devices: none -> 1.03 us  [cross(): lax.ppermute(block, 'seq', [(i, i ^ masks[i % 2]) for i in range(devices)])]
where the time goes in v3:
time: 21.6 us; the launch traced here: 21.4 us
  starting transfers between devices  10.5 us (49%)
  Pallas kernels  6.33 us (29%)
  waiting for transfers between devices  3.93 us (18%)
  between operations  0.69 us (3%)
    pallas_call x5, Pallas kernels, call(): pl.pallas_call(kernel, out_shape=outs, in_specs=[pl.BlockSpec(memory_spac...  6.33 us
    ppermute x4, starting transfers between devices, cross(): lax.ppermute(block, 'seq', [(i, i ^ masks[i % 2]) for i in range(devices)])  6.03 us
    ppermute x3, starting transfers between devices, swap(): return lax.ppermute(block, 'seq', [(i, i ^ mask) for i in range(devices)])  3.92 us
    ppermute x3, waiting for transfers between devices, swap(): return lax.ppermute(block, 'seq', [(i, i ^ mask) for i in range(devices)])  2.01 us
    ppermute x4, waiting for transfers between devices, cross(): lax.ppermute(block, 'seq', [(i, i ^ masks[i % 2]) for i in range(devices)])  1.03 us
    ppermute x1, waiting for transfers between devices, chain(): return lax.ppermute(block, 'seq', route)  0.89 us
    ppermute x1, starting transfers between devices, chain(): return lax.ppermute(block, 'seq', route)  0.51 us
  transfers between devices with their start and end apart: 8, of which 4 were waited for; matrix products, arithmetic and copies ran while one was open for 0% of the time, Pallas kernels for 12%

profile of v3, /device:TPU:0, one launch (start us, length us, event | category | flops | bytes accessed | tf_op | source)
XLA Modules:
  0.0 21.4 jit_solution(9012877615097761797)
XLA Ops:
  0.6 1.3 %shard_map.131 = (bf16[128,256]{1,0:T(8,128)(2,1)S(1)}, bf16[128,256]{1,0:T(8,128)(2,1)S(1)}, bf16[128,256]{1,0:T(8,128)(2,1)S(1)}, bf16[256,256]{1,0:T(8,128)(2...) custom-call(bf16[128,256]{1,0:T(8,128)(2,1)} %tokens.1, ...), custom_call_target="tpu_custom_call" | custom-call | bytes 4194304 | tf_op jit(solution)/shard_map/pallas_call | solution.py:26
  2.0 0.5 %collective-permute-start = (bf16[128,256]{1,0:T(8,128)(2,1)S(1)}, bf16[128,256]{1,0:T(8,128)(2,1)S(1)}, u32[]{:S(2)}, u32[]{:S(2)}) collective-permute-start(bf16[128,256]{1,0:T(8,128)(2,1)S(1)} %get-tuple-element.32.product), channel_id=1, source_target_pairs={{1,2},{3,4},{5,6},{7,8},{9,10},{11,12},{13,14},{4,3},{6,5},{8,7},{... | collective-permute-start | bytes 196616 | tf_op jit(solution)/shard_map/ppermute | solution.py:291
  2.5 2.6 %collective-permute-start.1 = (bf16[128,256]{1,0:T(8,128)(2,1)S(1)}, bf16[128,256]{1,0:T(8,128)(2,1)S(1)}, u32[]{:S(2)}, u32[]{:S(2)}) collective-permute-start(bf16[128,256]{1,0:T(8,128)(2,1)S(1)} %get-tuple-element.32.product), channel_id=1, source_target_pairs={{0,1},{1,0},{2,3},{3,2},{4,5},{5,4},{6,7},{7,6},{8,9},{9,8},{10,11... | collective-permute-start | bytes 196616 | tf_op jit(solution)/shard_map/ppermute | solution.py:280
  5.1 1.2 %shard_map.132 = (f32[128,256]{1,0:T(8,128)S(1)}, f32[128,256]{1,0:T(8,128)S(1)}, f32[128,256]{1,0:T(8,128)S(1)}, f32[128,256]{1,0:T(8,128)S(1)}, f32[16,256]{1,...) custom-call(bf16[128,256]{1,0:T(8,128)(2,1)S(1)} %get-tuple-element., ...), custom_call_target="tpu_custom_call" | custom-call | bytes 4194304 | tf_op jit(solution)/shard_map/pallas_call | solution.py:26
  6.3 0.9 %collective-permute-done.rim_chain = bf16[128,256]{1,0:T(8,128)(2,1)S(1)} collective-permute-done((bf16[128,256]{1,0:T(8,128)(2,1)S(1)}, bf16[128,256]{1,0:T(8,128)(2,1)S(1)}, u32[]{:S(2)}, u32[]{:S(2)}) %collective-permute-start) | collective-permute-done | bytes 65568 | tf_op jit(solution)/shard_map/ppermute | solution.py:291
  7.2 0.0 collective-permute-done.1.rim_pair
  7.2 1.5 %shard_map.133 = (bf16[128,256]{1,0:T(8,128)(2,1)S(1)}, f32[128,256]{1,0:T(8,128)S(1)}, bf16[128,256]{1,0:T(8,128)(2,1)S(1)}, f32[16,256]{1,0:T(8,128)S(1)}) custom-call(f32[128,256]{1,0:T(8,128)S(1)} %get-tuple-element.40.near, bf16[128,256]{1,0:T(8,128)(2,1)S(1)} %collective-permute-done.rim_chain, bf16[128,256]{1,0:T(8,128)(2,1)S(1)} %collective-permute-done.1.rim_pair, ...), custom_call_target="tpu_custom_call" | custom-call | bytes 4194304 | tf_op jit(solution)/shard_map/pallas_call | solution.py:26
  8.7 0.1 collective-permute-start.2
  8.8 1.2 %collective-permute-done.2 = f32[16,256]{1,0:T(8,128)S(1)} collective-permute-done((f32[16,256]{1,0:T(8,128)S(1)}, f32[16,256]{1,0:T(8,128)S(1)}, u32[]{:S(2)}, u32[]{:S(2)}) %collective-permute-start.2) | collective-permute-done | bytes 16416 | tf_op jit(solution)/shard_map/ppermute | solution.py:280
  10.0 4.3 %collective-permute-start.3 = (f32[16,256]{1,0:T(8,128)S(1)}, f32[16,256]{1,0:T(8,128)S(1)}, u32[]{:S(2)}, u32[]{:S(2)}) collective-permute-start(f32[16,256]{1,0:T(8,128)S(1)} %fusion.4), channel_id=1, source_target_pairs={{0,15},{1,12},{2,13},{3,14},{4,11},{5,8},{6,9},{7,10},{8,7},{9,4},... | collective-permute-start | bytes 49160 | tf_op jit(solution)/shard_map/ppermute | solution.py:296
  14.2 0.0 collective-permute-start.4
  14.2 0.6 %collective-permute-start.5 = (f32[16,256]{1,0:T(8,128)S(1)}, f32[16,256]{1,0:T(8,128)S(1)}, u32[]{:S(2)}, u32[]{:S(2)}) collective-permute-start(f32[16,256]{1,0:T(8,128)S(1)} %fusion.4), channel_id=1, source_target_pairs={{0,7},{1,4},{2,5},{3,6},{4,3},{5,0},{6,1},{7,2},{8,15},{9,12},{10,... | collective-permute-start | bytes 49160 | tf_op jit(solution)/shard_map/ppermute | solution.py:296
  14.9 1.2 %collective-permute-start.6 = (f32[16,256]{1,0:T(8,128)S(1)}, f32[16,256]{1,0:T(8,128)S(1)}, u32[]{:S(2)}, u32[]{:S(2)}) collective-permute-start(f32[16,256]{1,0:T(8,128)S(1)} %fusion.4), channel_id=1, source_target_pairs={{0,3},{1,2},{2,1},{3,0},{4,7},{5,6},{6,5},{7,4},{8,11},{9,10},{10,... | collective-permute-start | bytes 49160 | tf_op jit(solution)/shard_map/ppermute | solution.py:296
  16.0 1.3 %shard_map.134 = (f32[128,256]{1,0:T(8,128)S(1)}, f32[128,256]{1,0:T(8,128)S(1)}, bf16[128,256]{1,0:T(8,128)(2,1)}) custom-call(f32[128,256]{1,0:T(8,128)S(1)} %get-tuple-element.49.signal, f32[16,256]{1,0:T(8,128)S(1)} %get-tuple-element.50.weights, f32[16,8,256]{2,1,0:T(8,128)S(1)} %get-tuple-element.51.rise, f32[16,256]{1,0:T(8,128)S(1)} %get-tuple-element.47.fade, ...), custom_call_target="tpu_custom_call" | custom-call | bytes 4194304 | tf_op jit(solution)/shard_map/pallas_call | solution.py:26
  17.3 0.0 collective-permute-done.3
  17.4 1.0 %collective-permute-done.4 = f32[16,256]{1,0:T(8,128)S(1)} collective-permute-done((f32[16,256]{1,0:T(8,128)S(1)}, f32[16,256]{1,0:T(8,128)S(1)}, u32[]{:S(2)}, u32[]{:S(2)}) %collective-permute-start.4) | collective-permute-done | bytes 16416 | tf_op jit(solution)/shard_map/ppermute | solution.py:296
  18.4 0.0 collective-permute-done.5
  18.4 0.0 collective-permute-done.6
  18.4 1.2 %collective-permute-start.7 = (f32[16,256]{1,0:T(8,128)S(1)}, f32[16,256]{1,0:T(8,128)S(1)}, u32[]{:S(2)}, u32[]{:S(2)}) collective-permute-start(f32[16,256]{1,0:T(8,128)S(1)} %fusion.1), channel_id=1, source_target_pairs={{0,1},{1,0},{2,3},{3,2},{4,5},{5,4},{6,7},{7,6},{8,9},{9,8},{10,11... | collective-permute-start | bytes 49160 | tf_op jit(solution)/shard_map/ppermute | solution.py:280
  19.6 0.8 %collective-permute-done.7 = f32[16,256]{1,0:T(8,128)S(1)} collective-permute-done((f32[16,256]{1,0:T(8,128)S(1)}, f32[16,256]{1,0:T(8,128)S(1)}, u32[]{:S(2)}, u32[]{:S(2)}) %collective-permute-start.7) | collective-permute-done | bytes 16416 | tf_op jit(solution)/shard_map/ppermute | solution.py:280
  20.5 0.9 %shard_map.135 = bf16[128,256]{1,0:T(8,128)(2,1)} custom-call(f32[128,256]{1,0:T(8,128)S(1)} %get-tuple-element.58.near, f32[16,256]{1,0:T(8,128)S(1)} %fusion.carry, f32[16,8,256]{2,1,0:T(8,128)S(1)} %get-tuple-element.51.rise, f32[16,256]{1,0:T(8,128)S(1)} %get-tuple-element.47.fade, f32[128,256]{1,0:T(8,128)S(1)} %get-tuple-element.60.queries, ...), custom_call_target="tpu_custom_call" | custom-call | bytes 4194304 | tf_op jit(solution)/shard_map/pallas_call | solution.py:26
  (3 shorter events, 0.0 us)
Async XLA Ops:
  2.0 5.2 %collective-permute-start = (bf16[128,256]{1,0:T(8,128)(2,1)S(1)}, bf16[128,256]{1,0:T(8,128)(2,1)S(1)}, u32[]{:S(2)}, u32[]{:S(2)}) collective-permute-start(bf16[128,256]{1,0:T(8,128)(2,1)S(1)} %get-tuple-element.32.product), channel_id=1, source_target_pairs={{1,2},{3,4},{5,6},{7,8},{9,10},{11,12},{13,14},{4,3},{6,5},{8,7},{... | collective-permute-start | bytes 196616 | tf_op jit(solution)/shard_map/ppermute | solution.py:291
  2.5 4.7 %collective-permute-start.1 = (bf16[128,256]{1,0:T(8,128)(2,1)S(1)}, bf16[128,256]{1,0:T(8,128)(2,1)S(1)}, u32[]{:S(2)}, u32[]{:S(2)}) collective-permute-start(bf16[128,256]{1,0:T(8,128)(2,1)S(1)} %get-tuple-element.32.product), channel_id=1, source_target_pairs={{0,1},{1,0},{2,3},{3,2},{4,5},{5,4},{6,7},{7,6},{8,9},{9,8},{10,11... | collective-permute-start | bytes 196616 | tf_op jit(solution)/shard_map/ppermute | solution.py:280
  8.7 1.2 %collective-permute-start.2 = (f32[16,256]{1,0:T(8,128)S(1)}, f32[16,256]{1,0:T(8,128)S(1)}, u32[]{:S(2)}, u32[]{:S(2)}) collective-permute-start(f32[16,256]{1,0:T(8,128)S(1)} %get-tuple-element.55), channel_id=1, source_target_pairs={{0,1},{1,0},{2,3},{3,2},{4,5},{5,4},{6,7},{7,6},{8,9},{9,8},{10,11... | collective-permute-start | bytes 49160 | tf_op jit(solution)/shard_map/ppermute | solution.py:280
  10.0 7.4 %collective-permute-start.3 = (f32[16,256]{1,0:T(8,128)S(1)}, f32[16,256]{1,0:T(8,128)S(1)}, u32[]{:S(2)}, u32[]{:S(2)}) collective-permute-start(f32[16,256]{1,0:T(8,128)S(1)} %fusion.4), channel_id=1, source_target_pairs={{0,15},{1,12},{2,13},{3,14},{4,11},{5,8},{6,9},{7,10},{8,7},{9,4},... | collective-permute-start | bytes 49160 | tf_op jit(solution)/shard_map/ppermute | solution.py:296
  14.2 4.1 %collective-permute-start.4 = (f32[16,256]{1,0:T(8,128)S(1)}, f32[16,256]{1,0:T(8,128)S(1)}, u32[]{:S(2)}, u32[]{:S(2)}) collective-permute-start(f32[16,256]{1,0:T(8,128)S(1)} %fusion.4), channel_id=1, source_target_pairs={{0,11},{1,8},{2,9},{3,10},{4,15},{5,12},{6,13},{7,14},{8,3},{9,0},... | collective-permute-start | bytes 49160 | tf_op jit(solution)/shard_map/ppermute | solution.py:296
  14.2 4.1 %collective-permute-start.5 = (f32[16,256]{1,0:T(8,128)S(1)}, f32[16,256]{1,0:T(8,128)S(1)}, u32[]{:S(2)}, u32[]{:S(2)}) collective-permute-start(f32[16,256]{1,0:T(8,128)S(1)} %fusion.4), channel_id=1, source_target_pairs={{0,7},{1,4},{2,5},{3,6},{4,3},{5,0},{6,1},{7,2},{8,15},{9,12},{10,... | collective-permute-start | bytes 49160 | tf_op jit(solution)/shard_map/ppermute | solution.py:296
  14.9 3.5 %collective-permute-start.6 = (f32[16,256]{1,0:T(8,128)S(1)}, f32[16,256]{1,0:T(8,128)S(1)}, u32[]{:S(2)}, u32[]{:S(2)}) collective-permute-start(f32[16,256]{1,0:T(8,128)S(1)} %fusion.4), channel_id=1, source_target_pairs={{0,3},{1,2},{2,1},{3,0},{4,7},{5,6},{6,5},{7,4},{8,11},{9,10},{10,... | collective-permute-start | bytes 49160 | tf_op jit(solution)/shard_map/ppermute | solution.py:296
  18.4 2.1 %collective-permute-start.7 = (f32[16,256]{1,0:T(8,128)S(1)}, f32[16,256]{1,0:T(8,128)S(1)}, u32[]{:S(2)}, u32[]{:S(2)}) collective-permute-start(f32[16,256]{1,0:T(8,128)S(1)} %fusion.1), channel_id=1, source_target_pairs={{0,1},{1,0},{2,3},{3,2},{4,5},{5,4},{6,7},{7,6},{8,9},{9,8},{10,11... | collective-permute-start | bytes 49160 | tf_op jit(solution)/shard_map/ppermute | solution.py:280

commit v4 on v3

--- a/solution.py
+++ b/solution.py
@@ -11,8 +11,7 @@
 BF16 = jnp.bfloat16
 LANES = 128
 SUB = 8
-TAP_GROUP = 4
-STEP = SUB * TAP_GROUP
+TILE_GROUP = 4
 VMEM_LIMIT = 32 * 1024 * 1024
 WORK = 4 * 1024 * 1024
 
@@ -48,46 +47,55 @@
     return jnp.dot(left, right, preferred_element_type=F32)
 
 
-def shifted_copies(values, store, lead):
+def repeat_rows(taps, wide):
+    for j in range(taps.shape[0]):
+        wide[j] = jnp.broadcast_to(taps[j : j + 1, :], wide.shape[1:])
+
+
+def tap_sums(values, wide, total, rim):
     rows, width = values.shape
-    tail = store.shape[1] - lead - rows
-    if tail:
-        values = jnp.concatenate([values, jnp.zeros((tail, width), F32)], 0)
-    if lead:
-        values = jnp.concatenate([jnp.zeros((lead, width), F32), values], 0)
-    store[0] = values
-    for r in range(1, SUB):
-        store[r] = pltpu.roll(values, r, 0)
-
-
-def tap_sum(taps, store, group, base, size):
-    width = store.shape[2]
-
-    def body(step, total):
-        first = pl.multiple_of(base - step * SUB, SUB)
-        for r in range(SUB):
-            tap = taps[pl.ds((group * TAP_GROUP + step) * SUB + r, 1), :]
-            total = total + tap * store[r, pl.ds(first, size), :]
-        return total
-
-    return lax.fori_loop(0, TAP_GROUP, body, jnp.zeros((size, width), F32))
-
-
-def own_taps(values, taps, store, total):
-    rows = values.shape[0]
-    shifted_copies(values, store, STEP)
-    total[...] = tap_sum(taps, store, 0, STEP, rows)
-    for group in range(1, rows // STEP):
-        skip = group * STEP
-        total[pl.ds(skip, rows - skip), :] += tap_sum(taps, store, group, STEP, rows - skip)
-
-
-def rim_taps(values, taps, store, total):
-    rows = values.shape[0]
-    shifted_copies(values, store, 0)
-    for group in range(rows // STEP):
-        size = (group + 1) * STEP
-        total[pl.ds(0, size), :] += tap_sum(taps, store, group, rows - group * STEP, size)
+    tiles = rows // SUB
+    row_ids = lax.broadcasted_iota(jnp.int32, (SUB, LANES), 0)
+    start = -1 if rim else 0
+
+    def column(at, carried):
+        here = pl.ds(pl.multiple_of(at * LANES, LANES), LANES)
+        above = None
+        for first in range(start, start + tiles, TILE_GROUP):
+            places = range(first, min(first + TILE_GROUP, start + tiles))
+            sums = {}
+            for q in range(tiles):
+                used = [a for a in places if (q > a if rim else q <= a)]
+                if not used:
+                    continue
+                taps = [wide[q * SUB + r, :, here] for r in range(SUB)]
+                for a in used:
+                    tile = (tiles if rim else 0) + a - q
+                    value = values[tile * SUB : (tile + 1) * SUB, here]
+                    terms = [tap * value for tap in taps]
+                    old = sums.get(a)
+                    sums[a] = terms if old is None else [x + y for x, y in zip(old, terms)]
+            for a in places:
+                turned = sums[a][:1]
+                turned += [pltpu.roll(sums[a][r], r, 0) for r in range(1, SUB)]
+                if a >= 0:
+                    add_tile(a, here, turned, above)
+                above = turned
+        if rim:
+            add_tile(tiles - 1, here, None, above)
+        return carried
+
+    def add_tile(a, here, turned, above):
+        parts = [] if turned is None else turned[:1]
+        for r in range(1, SUB):
+            low = 0.0 if turned is None else turned[r]
+            high = 0.0 if above is None else above[r]
+            parts.append(jnp.where(row_ids < r, high, low))
+        while len(parts) > 1:
+            parts = [functools.reduce(jnp.add, parts[i : i + 2]) for i in range(0, len(parts), 2)]
+        total[a * SUB : (a + 1) * SUB, here] += parts[0]
+
+    lax.fori_loop(0, width // LANES, column, 0)
 
 
 def fetches(pairs, sems):
@@ -131,13 +139,15 @@
 def near_kernel(
     devices, product, normed, proj_q, taps, rates, residues, inv_rms, gain, out_a, out_b, proj,
     total, queries, taps_wide, scale, weights, rise, fall, fade, shares, out_a_in, out_b_in, proj_in,
-    store, sems,
+    values, sems,
 ):
     copies = fetches([(out_a, out_a_in), (proj, proj_in), (out_b, out_b_in)], sems)
     rows, width = product.shape
     modes = rates.shape[0]
-    taps_wide[...] = taps[...].astype(F32)
-    own_taps(product[...].astype(F32), taps_wide, store, total)
+    repeat_rows(taps[...].astype(F32), taps_wide)
+    values[...] = product[...].astype(F32)
+    total[...] = jnp.zeros_like(total)
+    tap_sums(values, taps_wide, total, rim=False)
     queries[...] = dot(normed[...], proj_q[...])
     scale[...] = spread(inv_rms[...], width) * gain[...]
     rate = rates[...]
@@ -159,14 +169,15 @@
 
 def middle_kernel(
     near, rim_chain, rim_pair, taps, queries, out_a, tokens, scale, proj, fade, fall,
-    partial, signal, normed_b, state, store, total,
+    partial, signal, normed_b, state, values, total,
 ):
     width = near.shape[1]
     modes = fade.shape[0]
     me = lax.axis_index("seq")
     total[...] = near[...]
     rim = jnp.where(me % 2 == 1, rim_pair[...].astype(F32), rim_chain[...].astype(F32))
-    rim_taps(jnp.where(me == 0, 0.0, rim), taps, store, total)
+    values[...] = jnp.where(me == 0, 0.0, rim)
+    tap_sums(values, taps, total, rim=True)
     gated = (queries[...] * total[...]).astype(BF16)
     term = dot(gated, out_a[...]).astype(BF16)
     partial[...] = term
@@ -188,7 +199,7 @@
 
 def local_kernel(
     signal, weights, rise, fade, normed, proj, partial,
-    total, queries, partial_out, response, store, sems,
+    total, queries, partial_out, response, wide, sems,
 ):
     copies = fetches([(partial, partial_out)], sems)
     rows, width = signal.shape
@@ -200,7 +211,9 @@
             add_fading(sums, weights[m : m + 1, here] * rise[m, :, here], fade[m : m + 1, here])
         for i, part in enumerate(sums):
             response[i * SUB : (i + 1) * SUB, here] = part
-    own_taps(signal[...], response, store, total)
+    repeat_rows(response[...], wide)
+    total[...] = jnp.zeros_like(total)
+    tap_sums(signal, wide, total, rim=False)
     queries[...] = dot(normed[...], proj[:, :width])
     for copy in copies:
         copy.wait()
@@ -337,7 +350,7 @@
     taps = taps_a.shape[0]
     modes = rates_b.shape[0]
     devices = lax.axis_size("seq")
-    assert taps == rows and rows % STEP == 0 and devices > 2
+    assert taps == rows and rows % SUB == 0 and devices > 2
     wide = pltpu.VMEM((rows, width), F32)
     narrow = pltpu.VMEM((rows, width), BF16)
     square = pltpu.VMEM((width, width), BF16)
@@ -345,7 +358,7 @@
     states = pltpu.VMEM((modes, width), F32)
     by_token = pltpu.VMEM((1, rows), F32)
     by_channel = pltpu.VMEM((1, width), F32)
-    store = pltpu.VMEM((SUB, rows + STEP, width), F32)
+    spread_taps = pltpu.VMEM((taps, SUB, width), F32)
     semaphores = pltpu.SemaphoreType.DMA
 
     product, normed, tokens, proj_q, taps_a, rates, residues, inv_rms, gain = call(
@@ -364,21 +377,21 @@
     ) = call(
         functools.partial(near_kernel, devices),
         (
-            wide, wide, wide, wide, states, bank, bank, states, shares,
+            wide, wide, spread_taps, wide, states, bank, bank, states, shares,
             square, square, pltpu.VMEM(proj_b.shape, BF16),
         ),
-        (store, semaphores((3,))),
+        (wide, semaphores((3,))),
         product, normed, proj_q, taps_a, rates, residues, inv_rms, gain, [out_a], [out_b], [proj_b],
     )
 
     partial_a, signal, normed_b, state = call(
-        middle_kernel, (narrow, wide, narrow, states), (store, wide),
+        middle_kernel, (narrow, wide, narrow, states), (wide, wide),
         near, rim_chain, rim_pair, taps_wide, queries, out_a, tokens, scale, proj_b, fade, fall,
     )
     near_b, queries_b, partial_a = call(
         local_kernel,
         (wide, wide, pltpu.HBM((rows, width), BF16)),
-        (wide, store, semaphores((1,))),
+        (wide, spread_taps, semaphores((1,))),
         signal, weights, rise, fade, normed_b, proj_b, partial_a,
     )
     carry, near_b = carry_in(state, shares, near_b, devices)

time: 21.6 us -> 21.2 us (0.981)
  Pallas kernels: 6.33 us -> 5.62 us
  waiting for transfers between devices: 3.93 us -> 4.28 us
    pallas_call x5, Pallas kernels: 6.33 us -> 5.62 us  [call(): pl.pallas_call(kernel, out_shape=outs, in_specs=[pl.BlockSpec(memory_spac...]
    ppermute x4, waiting for transfers between devices: 1.03 us -> 1.27 us  [cross(): lax.ppermute(block, 'seq', [(i, i ^ masks[i % 2]) for i in range(devices)])]
  transfers between devices with their start and end apart: 8 -> 8, of which waited for: 4 -> 4; matrix products, arithmetic and copies ran while one was open for 0% -> 0% of each run, Pallas kernels for 12% -> 10%
where the time goes in v4:
time: 21.2 us; the launch traced here: 21.1 us
  starting transfers between devices  10.5 us (50%)
  Pallas kernels  5.62 us (27%)
  waiting for transfers between devices  4.28 us (20%)
  between operations  0.69 us (3%)
    ppermute x4, starting transfers between devices, cross(): lax.ppermute(block, 'seq', [(i, i ^ masks[i % 2]) for i in range(devices)])  6.03 us
    pallas_call x5, Pallas kernels, call(): pl.pallas_call(kernel, out_shape=outs, in_specs=[pl.BlockSpec(memory_spac...  5.62 us
    ppermute x3, starting transfers between devices, swap(): return lax.ppermute(block, 'seq', [(i, i ^ mask) for i in range(devices)])  3.92 us
    ppermute x3, waiting for transfers between devices, swap(): return lax.ppermute(block, 'seq', [(i, i ^ mask) for i in range(devices)])  2.01 us
    ppermute x4, waiting for transfers between devices, cross(): lax.ppermute(block, 'seq', [(i, i ^ masks[i % 2]) for i in range(devices)])  1.27 us
    ppermute x1, waiting for transfers between devices, chain(): return lax.ppermute(block, 'seq', route)  1 us
    ppermute x1, starting transfers between devices, chain(): return lax.ppermute(block, 'seq', route)  0.51 us
  transfers between devices with their start and end apart: 8, of which 4 were waited for; matrix products, arithmetic and copies ran while one was open for 0% of the time, Pallas kernels for 10%

profile of v4, /device:TPU:0, one launch (start us, length us, event | category | flops | bytes accessed | tf_op | source)
XLA Modules:
  0.0 21.1 jit_solution(17941162335982392904)
XLA Ops:
  0.6 1.3 %shard_map.131 = (bf16[128,256]{1,0:T(8,128)(2,1)S(1)}, bf16[128,256]{1,0:T(8,128)(2,1)S(1)}, bf16[128,256]{1,0:T(8,128)(2,1)S(1)}, bf16[256,256]{1,0:T(8,128)(2...) custom-call(bf16[128,256]{1,0:T(8,128)(2,1)} %tokens.1, ...), custom_call_target="tpu_custom_call" | custom-call | bytes 4194304 | tf_op jit(solution)/shard_map/pallas_call | solution.py:25
  2.0 0.5 %collective-permute-start = (bf16[128,256]{1,0:T(8,128)(2,1)S(1)}, bf16[128,256]{1,0:T(8,128)(2,1)S(1)}, u32[]{:S(2)}, u32[]{:S(2)}) collective-permute-start(bf16[128,256]{1,0:T(8,128)(2,1)S(1)} %get-tuple-element.32.product), channel_id=1, source_target_pairs={{1,2},{3,4},{5,6},{7,8},{9,10},{11,12},{13,14},{4,3},{6,5},{8,7},{... | collective-permute-start | bytes 196616 | tf_op jit(solution)/shard_map/ppermute | solution.py:304
  2.5 2.6 %collective-permute-start.1 = (bf16[128,256]{1,0:T(8,128)(2,1)S(1)}, bf16[128,256]{1,0:T(8,128)(2,1)S(1)}, u32[]{:S(2)}, u32[]{:S(2)}) collective-permute-start(bf16[128,256]{1,0:T(8,128)(2,1)S(1)} %get-tuple-element.32.product), channel_id=1, source_target_pairs={{0,1},{1,0},{2,3},{3,2},{4,5},{5,4},{6,7},{7,6},{8,9},{9,8},{10,11... | collective-permute-start | bytes 196616 | tf_op jit(solution)/shard_map/ppermute | solution.py:293
  5.1 1.1 %shard_map.132 = (f32[128,256]{1,0:T(8,128)S(1)}, f32[128,256]{1,0:T(8,128)S(1)}, f32[128,8,256]{2,1,0:T(8,128)S(1)}, f32[128,256]{1,0:T(8,128)S(1)}, f32[16,256...) custom-call(bf16[128,256]{1,0:T(8,128)(2,1)S(1)} %get-tuple-element., ...), custom_call_target="tpu_custom_call" | custom-call | bytes 4194304 | tf_op jit(solution)/shard_map/pallas_call | solution.py:25
  6.2 1.0 %collective-permute-done.rim_chain = bf16[128,256]{1,0:T(8,128)(2,1)S(1)} collective-permute-done((bf16[128,256]{1,0:T(8,128)(2,1)S(1)}, bf16[128,256]{1,0:T(8,128)(2,1)S(1)}, u32[]{:S(2)}, u32[]{:S(2)}) %collective-permute-start) | collective-permute-done | bytes 65568 | tf_op jit(solution)/shard_map/ppermute | solution.py:304
  7.2 0.0 collective-permute-done.1.rim_pair
  7.2 1.2 %shard_map.133 = (bf16[128,256]{1,0:T(8,128)(2,1)S(1)}, f32[128,256]{1,0:T(8,128)S(1)}, bf16[128,256]{1,0:T(8,128)(2,1)S(1)}, f32[16,256]{1,0:T(8,128)S(1)}) custom-call(f32[128,256]{1,0:T(8,128)S(1)} %get-tuple-element.40.near, bf16[128,256]{1,0:T(8,128)(2,1)S(1)} %collective-permute-done.rim_chain, bf16[128,256]{1,0:T(8,128)(2,1)S(1)} %collective-permute-done.1.rim_pair, ...), custom_call_target="tpu_custom_call" | custom-call | bytes 4194304 | tf_op jit(solution)/shard_map/pallas_call | solution.py:25
  8.4 0.1 collective-permute-start.2
  8.4 1.2 %collective-permute-done.2 = f32[16,256]{1,0:T(8,128)S(1)} collective-permute-done((f32[16,256]{1,0:T(8,128)S(1)}, f32[16,256]{1,0:T(8,128)S(1)}, u32[]{:S(2)}, u32[]{:S(2)}) %collective-permute-start.2) | collective-permute-done | bytes 16416 | tf_op jit(solution)/shard_map/ppermute | solution.py:293
  9.6 4.3 %collective-permute-start.3 = (f32[16,256]{1,0:T(8,128)S(1)}, f32[16,256]{1,0:T(8,128)S(1)}, u32[]{:S(2)}, u32[]{:S(2)}) collective-permute-start(f32[16,256]{1,0:T(8,128)S(1)} %fusion.4), channel_id=1, source_target_pairs={{0,15},{1,12},{2,13},{3,14},{4,11},{5,8},{6,9},{7,10},{8,7},{9,4},... | collective-permute-start | bytes 49160 | tf_op jit(solution)/shard_map/ppermute | solution.py:309
  13.9 0.0 collective-permute-start.4
  13.9 0.6 %collective-permute-start.5 = (f32[16,256]{1,0:T(8,128)S(1)}, f32[16,256]{1,0:T(8,128)S(1)}, u32[]{:S(2)}, u32[]{:S(2)}) collective-permute-start(f32[16,256]{1,0:T(8,128)S(1)} %fusion.4), channel_id=1, source_target_pairs={{0,7},{1,4},{2,5},{3,6},{4,3},{5,0},{6,1},{7,2},{8,15},{9,12},{10,... | collective-permute-start | bytes 49160 | tf_op jit(solution)/shard_map/ppermute | solution.py:309
  14.5 1.2 %collective-permute-start.6 = (f32[16,256]{1,0:T(8,128)S(1)}, f32[16,256]{1,0:T(8,128)S(1)}, u32[]{:S(2)}, u32[]{:S(2)}) collective-permute-start(f32[16,256]{1,0:T(8,128)S(1)} %fusion.4), channel_id=1, source_target_pairs={{0,3},{1,2},{2,1},{3,0},{4,7},{5,6},{6,5},{7,4},{8,11},{9,10},{10,... | collective-permute-start | bytes 49160 | tf_op jit(solution)/shard_map/ppermute | solution.py:309
  15.7 1.1 %shard_map.134 = (f32[128,256]{1,0:T(8,128)S(1)}, f32[128,256]{1,0:T(8,128)S(1)}, bf16[128,256]{1,0:T(8,128)(2,1)}) custom-call(f32[128,256]{1,0:T(8,128)S(1)} %get-tuple-element.49.signal, f32[16,256]{1,0:T(8,128)S(1)} %get-tuple-element.50.weights, f32[16,8,256]{2,1,0:T(8,128)S(1)} %get-tuple-element.51.rise, f32[16,256]{1,0:T(8,128)S(1)} %get-tuple-element.47.fade, ...), custom_call_target="tpu_custom_call" | custom-call | bytes 4194304 | tf_op jit(solution)/shard_map/pallas_call | solution.py:25
  16.7 0.0 collective-permute-done.3
  16.8 1.3 %collective-permute-done.4 = f32[16,256]{1,0:T(8,128)S(1)} collective-permute-done((f32[16,256]{1,0:T(8,128)S(1)}, f32[16,256]{1,0:T(8,128)S(1)}, u32[]{:S(2)}, u32[]{:S(2)}) %collective-permute-start.4) | collective-permute-done | bytes 16416 | tf_op jit(solution)/shard_map/ppermute | solution.py:309
  18.0 0.0 collective-permute-done.5
  18.0 0.0 collective-permute-done.6
  18.0 1.2 %collective-permute-start.7 = (f32[16,256]{1,0:T(8,128)S(1)}, f32[16,256]{1,0:T(8,128)S(1)}, u32[]{:S(2)}, u32[]{:S(2)}) collective-permute-start(f32[16,256]{1,0:T(8,128)S(1)} %fusion.1), channel_id=1, source_target_pairs={{0,1},{1,0},{2,3},{3,2},{4,5},{5,4},{6,7},{7,6},{8,9},{9,8},{10,11... | collective-permute-start | bytes 49160 | tf_op jit(solution)/shard_map/ppermute | solution.py:293
  19.3 0.8 %collective-permute-done.7 = f32[16,256]{1,0:T(8,128)S(1)} collective-permute-done((f32[16,256]{1,0:T(8,128)S(1)}, f32[16,256]{1,0:T(8,128)S(1)}, u32[]{:S(2)}, u32[]{:S(2)}) %collective-permute-start.7) | collective-permute-done | bytes 16416 | tf_op jit(solution)/shard_map/ppermute | solution.py:293
  20.1 0.9 %shard_map.135 = bf16[128,256]{1,0:T(8,128)(2,1)} custom-call(f32[128,256]{1,0:T(8,128)S(1)} %get-tuple-element.58.near, f32[16,256]{1,0:T(8,128)S(1)} %fusion.carry, f32[16,8,256]{2,1,0:T(8,128)S(1)} %get-tuple-element.51.rise, f32[16,256]{1,0:T(8,128)S(1)} %get-tuple-element.47.fade, f32[128,256]{1,0:T(8,128)S(1)} %get-tuple-element.60.queries, ...), custom_call_target="tpu_custom_call" | custom-call | bytes 4194304 | tf_op jit(solution)/shard_map/pallas_call | solution.py:25
  (3 shorter events, 0.0 us)
Async XLA Ops:
  2.0 5.2 %collective-permute-start = (bf16[128,256]{1,0:T(8,128)(2,1)S(1)}, bf16[128,256]{1,0:T(8,128)(2,1)S(1)}, u32[]{:S(2)}, u32[]{:S(2)}) collective-permute-start(bf16[128,256]{1,0:T(8,128)(2,1)S(1)} %get-tuple-element.32.product), channel_id=1, source_target_pairs={{1,2},{3,4},{5,6},{7,8},{9,10},{11,12},{13,14},{4,3},{6,5},{8,7},{... | collective-permute-start | bytes 196616 | tf_op jit(solution)/shard_map/ppermute | solution.py:304
  2.5 4.7 %collective-permute-start.1 = (bf16[128,256]{1,0:T(8,128)(2,1)S(1)}, bf16[128,256]{1,0:T(8,128)(2,1)S(1)}, u32[]{:S(2)}, u32[]{:S(2)}) collective-permute-start(bf16[128,256]{1,0:T(8,128)(2,1)S(1)} %get-tuple-element.32.product), channel_id=1, source_target_pairs={{0,1},{1,0},{2,3},{3,2},{4,5},{5,4},{6,7},{7,6},{8,9},{9,8},{10,11... | collective-permute-start | bytes 196616 | tf_op jit(solution)/shard_map/ppermute | solution.py:293
  8.4 1.2 %collective-permute-start.2 = (f32[16,256]{1,0:T(8,128)S(1)}, f32[16,256]{1,0:T(8,128)S(1)}, u32[]{:S(2)}, u32[]{:S(2)}) collective-permute-start(f32[16,256]{1,0:T(8,128)S(1)} %get-tuple-element.55), channel_id=1, source_target_pairs={{0,1},{1,0},{2,3},{3,2},{4,5},{5,4},{6,7},{7,6},{8,9},{9,8},{10,11... | collective-permute-start | bytes 49160 | tf_op jit(solution)/shard_map/ppermute | solution.py:293
  9.6 7.1 %collective-permute-start.3 = (f32[16,256]{1,0:T(8,128)S(1)}, f32[16,256]{1,0:T(8,128)S(1)}, u32[]{:S(2)}, u32[]{:S(2)}) collective-permute-start(f32[16,256]{1,0:T(8,128)S(1)} %fusion.4), channel_id=1, source_target_pairs={{0,15},{1,12},{2,13},{3,14},{4,11},{5,8},{6,9},{7,10},{8,7},{9,4},... | collective-permute-start | bytes 49160 | tf_op jit(solution)/shard_map/ppermute | solution.py:309
  13.9 4.1 %collective-permute-start.4 = (f32[16,256]{1,0:T(8,128)S(1)}, f32[16,256]{1,0:T(8,128)S(1)}, u32[]{:S(2)}, u32[]{:S(2)}) collective-permute-start(f32[16,256]{1,0:T(8,128)S(1)} %fusion.4), channel_id=1, source_target_pairs={{0,11},{1,8},{2,9},{3,10},{4,15},{5,12},{6,13},{7,14},{8,3},{9,0},... | collective-permute-start | bytes 49160 | tf_op jit(solution)/shard_map/ppermute | solution.py:309
  13.9 4.1 %collective-permute-start.5 = (f32[16,256]{1,0:T(8,128)S(1)}, f32[16,256]{1,0:T(8,128)S(1)}, u32[]{:S(2)}, u32[]{:S(2)}) collective-permute-start(f32[16,256]{1,0:T(8,128)S(1)} %fusion.4), channel_id=1, source_target_pairs={{0,7},{1,4},{2,5},{3,6},{4,3},{5,0},{6,1},{7,2},{8,15},{9,12},{10,... | collective-permute-start | bytes 49160 | tf_op jit(solution)/shard_map/ppermute | solution.py:309
  14.5 3.5 %collective-permute-start.6 = (f32[16,256]{1,0:T(8,128)S(1)}, f32[16,256]{1,0:T(8,128)S(1)}, u32[]{:S(2)}, u32[]{:S(2)}) collective-permute-start(f32[16,256]{1,0:T(8,128)S(1)} %fusion.4), channel_id=1, source_target_pairs={{0,3},{1,2},{2,1},{3,0},{4,7},{5,6},{6,5},{7,4},{8,11},{9,10},{10,... | collective-permute-start | bytes 49160 | tf_op jit(solution)/shard_map/ppermute | solution.py:309
  18.0 2.1 %collective-permute-start.7 = (f32[16,256]{1,0:T(8,128)S(1)}, f32[16,256]{1,0:T(8,128)S(1)}, u32[]{:S(2)}, u32[]{:S(2)}) collective-permute-start(f32[16,256]{1,0:T(8,128)S(1)} %fusion.1), channel_id=1, source_target_pairs={{0,1},{1,0},{2,3},{3,2},{4,5},{5,4},{6,7},{7,6},{8,9},{9,8},{10,11... | collective-permute-start | bytes 49160 | tf_op jit(solution)/shard_map/ppermute | solution.py:293

commit v5 on v4

--- a/solution.py
+++ b/solution.py
@@ -59,7 +59,7 @@
     start = -1 if rim else 0
 
     def column(at, carried):
-        here = pl.ds(pl.multiple_of(at * LANES, LANES), LANES)
+        here = pl.ds(at * LANES, LANES)
         above = None
         for first in range(start, start + tiles, TILE_GROUP):
             places = range(first, min(first + TILE_GROUP, start + tiles))
@@ -95,7 +95,8 @@
             parts = [functools.reduce(jnp.add, parts[i : i + 2]) for i in range(0, len(parts), 2)]
         total[a * SUB : (a + 1) * SUB, here] += parts[0]
 
-    lax.fori_loop(0, width // LANES, column, 0)
+    for at in range(width // LANES):
+        column(at, 0)
 
 
 def fetches(pairs, sems):
@@ -266,7 +267,8 @@
 
 
 def routes(radix):
-    return [(k + 1, k) for k in range(radix - 2, 0, -2)] + [(1, 1)]
+    pairs = {8: [(5, 4), (7, 6), (3, 2)], 4: [(3, 2)], 2: []}
+    return pairs[radix] + [(1, 1)]
 
 
 def share_plan(me, devices, rows):
@@ -304,9 +306,14 @@
     return lax.ppermute(block, "seq", route)
 
 
-def cross(block, devices, stride, even, odd):
-    masks = (even * stride + 1, odd * stride + 1)
-    return lax.ppermute(block, "seq", [(i, i ^ masks[i % 2]) for i in range(devices)])
+def cross(block, devices, stride, radix, even, odd):
+    route = []
+    for i in range(devices):
+        mask = (even, odd)[i % 2]
+        place = i // stride % radix
+        short = stride * radix == devices and mask & 6 == 6 and place & 4
+        route.append((i, i ^ ((mask ^ 2 if short else mask) * stride + 1)))
+    return lax.ppermute(block, "seq", route)
 
 
 def carry_in(state, shares, near, devices):
@@ -315,7 +322,7 @@
     total = state * next(share) + beside * next(share)
     before = None
     for stride, radix in levels(devices):
-        parts = [cross(total, devices, stride, even, odd) for even, odd in routes(radix)]
+        parts = [cross(total, devices, stride, radix, even, odd) for even, odd in routes(radix)]
         last = stride * radix == devices
         sums, totals = [], []
         for part in parts:

time: 21.2 us -> 20.9 us (0.986)
  Pallas kernels: 5.62 us -> 5.34 us
    pallas_call x5, Pallas kernels: 5.62 us -> 5.34 us  [call(): pl.pallas_call(kernel, out_shape=outs, in_specs=[pl.BlockSpec(memory_spac...]
  transfers between devices with their start and end apart: 8 -> 8, of which waited for: 4 -> 5; matrix products, arithmetic and copies ran while one was open for 0% -> 0% of each run, Pallas kernels for 10% -> 10%
where the time goes in v5:
time: 20.9 us; the launch traced here: 20.8 us
  starting transfers between devices  10.5 us (50%)
  Pallas kernels  5.34 us (26%)
  waiting for transfers between devices  4.24 us (20%)
  between operations  0.69 us (3%)
    ppermute x4, starting transfers between devices, cross(): return lax.ppermute(block, 'seq', route)  5.97 us
    pallas_call x5, Pallas kernels, call(): pl.pallas_call(kernel, out_shape=outs, in_specs=[pl.BlockSpec(memory_spac...  5.34 us
    ppermute x3, starting transfers between devices, swap(): return lax.ppermute(block, 'seq', [(i, i ^ mask) for i in range(devices)])  4 us
    ppermute x3, waiting for transfers between devices, swap(): return lax.ppermute(block, 'seq', [(i, i ^ mask) for i in range(devices)])  2.01 us
    ppermute x4, waiting for transfers between devices, cross(): return lax.ppermute(block, 'seq', route)  1.23 us
    ppermute x1, waiting for transfers between devices, chain(): return lax.ppermute(block, 'seq', route)  0.99 us
    ppermute x1, starting transfers between devices, chain(): return lax.ppermute(block, 'seq', route)  0.51 us
  transfers between devices with their start and end apart: 8, of which 5 were waited for; matrix products, arithmetic and copies ran while one was open for 0% of the time, Pallas kernels for 10%

profile of v5, /device:TPU:0, one launch (start us, length us, event | category | flops | bytes accessed | tf_op | source)
XLA Modules:
  0.0 20.8 jit_solution(835563847092273938)
XLA Ops:
  0.6 1.3 %shard_map.131 = (bf16[128,256]{1,0:T(8,128)(2,1)S(1)}, bf16[128,256]{1,0:T(8,128)(2,1)S(1)}, bf16[128,256]{1,0:T(8,128)(2,1)S(1)}, bf16[256,256]{1,0:T(8,128)(2...) custom-call(bf16[128,256]{1,0:T(8,128)(2,1)} %tokens.1, ...), custom_call_target="tpu_custom_call" | custom-call | bytes 4194304 | tf_op jit(solution)/shard_map/pallas_call | solution.py:25
  2.0 0.5 %collective-permute-start = (bf16[128,256]{1,0:T(8,128)(2,1)S(1)}, bf16[128,256]{1,0:T(8,128)(2,1)S(1)}, u32[]{:S(2)}, u32[]{:S(2)}) collective-permute-start(bf16[128,256]{1,0:T(8,128)(2,1)S(1)} %get-tuple-element.32.product), channel_id=1, source_target_pairs={{1,2},{3,4},{5,6},{7,8},{9,10},{11,12},{13,14},{4,3},{6,5},{8,7},{... | collective-permute-start | bytes 196616 | tf_op jit(solution)/shard_map/ppermute | solution.py:306
  2.5 2.6 %collective-permute-start.1 = (bf16[128,256]{1,0:T(8,128)(2,1)S(1)}, bf16[128,256]{1,0:T(8,128)(2,1)S(1)}, u32[]{:S(2)}, u32[]{:S(2)}) collective-permute-start(bf16[128,256]{1,0:T(8,128)(2,1)S(1)} %get-tuple-element.32.product), channel_id=1, source_target_pairs={{0,1},{1,0},{2,3},{3,2},{4,5},{5,4},{6,7},{7,6},{8,9},{9,8},{10,11... | collective-permute-start | bytes 196616 | tf_op jit(solution)/shard_map/ppermute | solution.py:295
  5.1 1.1 %shard_map.132 = (f32[128,256]{1,0:T(8,128)S(1)}, f32[128,256]{1,0:T(8,128)S(1)}, f32[128,8,256]{2,1,0:T(8,128)S(1)}, f32[128,256]{1,0:T(8,128)S(1)}, f32[16,256...) custom-call(bf16[128,256]{1,0:T(8,128)(2,1)S(1)} %get-tuple-element., ...), custom_call_target="tpu_custom_call" | custom-call | bytes 4194304 | tf_op jit(solution)/shard_map/pallas_call | solution.py:25
  6.2 1.0 %collective-permute-done.rim_chain = bf16[128,256]{1,0:T(8,128)(2,1)S(1)} collective-permute-done((bf16[128,256]{1,0:T(8,128)(2,1)S(1)}, bf16[128,256]{1,0:T(8,128)(2,1)S(1)}, u32[]{:S(2)}, u32[]{:S(2)}) %collective-permute-start) | collective-permute-done | bytes 65568 | tf_op jit(solution)/shard_map/ppermute | solution.py:306
  7.2 0.0 collective-permute-done.1.rim_pair
  7.2 1.1 %shard_map.133 = (bf16[128,256]{1,0:T(8,128)(2,1)S(1)}, f32[128,256]{1,0:T(8,128)S(1)}, bf16[128,256]{1,0:T(8,128)(2,1)S(1)}, f32[16,256]{1,0:T(8,128)S(1)}) custom-call(f32[128,256]{1,0:T(8,128)S(1)} %get-tuple-element.40.near, bf16[128,256]{1,0:T(8,128)(2,1)S(1)} %collective-permute-done.rim_chain, bf16[128,256]{1,0:T(8,128)(2,1)S(1)} %collective-permute-done.1.rim_pair, ...), custom_call_target="tpu_custom_call" | custom-call | bytes 4194304 | tf_op jit(solution)/shard_map/pallas_call | solution.py:25
  8.3 0.1 collective-permute-start.2
  8.3 1.2 %collective-permute-done.2 = f32[16,256]{1,0:T(8,128)S(1)} collective-permute-done((f32[16,256]{1,0:T(8,128)S(1)}, f32[16,256]{1,0:T(8,128)S(1)}, u32[]{:S(2)}, u32[]{:S(2)}) %collective-permute-start.2) | collective-permute-done | bytes 16416 | tf_op jit(solution)/shard_map/ppermute | solution.py:295
  9.5 3.9 %collective-permute-start.3 = (f32[16,256]{1,0:T(8,128)S(1)}, f32[16,256]{1,0:T(8,128)S(1)}, u32[]{:S(2)}, u32[]{:S(2)}) collective-permute-start(f32[16,256]{1,0:T(8,128)S(1)} %fusion.4), channel_id=1, source_target_pairs={{0,11},{1,8},{2,9},{3,10},{4,15},{5,12},{6,13},{7,14},{8,3},{9,0},... | collective-permute-start | bytes 49160 | tf_op jit(solution)/shard_map/ppermute | solution.py:316
  13.4 1.1 %collective-permute-start.4 = (f32[16,256]{1,0:T(8,128)S(1)}, f32[16,256]{1,0:T(8,128)S(1)}, u32[]{:S(2)}, u32[]{:S(2)}) collective-permute-start(f32[16,256]{1,0:T(8,128)S(1)} %fusion.4), channel_id=1, source_target_pairs={{0,15},{1,12},{2,13},{3,14},{4,11},{5,8},{6,9},{7,10},{8,3},{9,0},... | collective-permute-start | bytes 49160 | tf_op jit(solution)/shard_map/ppermute | solution.py:316
  14.4 0.0 collective-permute-start.5
  14.5 1.0 %collective-permute-start.6 = (f32[16,256]{1,0:T(8,128)S(1)}, f32[16,256]{1,0:T(8,128)S(1)}, u32[]{:S(2)}, u32[]{:S(2)}) collective-permute-start(f32[16,256]{1,0:T(8,128)S(1)} %fusion.4), channel_id=1, source_target_pairs={{0,3},{1,2},{2,1},{3,0},{4,7},{5,6},{6,5},{7,4},{8,11},{9,10},{10,... | collective-permute-start | bytes 49160 | tf_op jit(solution)/shard_map/ppermute | solution.py:316
  15.5 0.9 %shard_map.134 = (f32[128,256]{1,0:T(8,128)S(1)}, f32[128,256]{1,0:T(8,128)S(1)}, bf16[128,256]{1,0:T(8,128)(2,1)}) custom-call(f32[128,256]{1,0:T(8,128)S(1)} %get-tuple-element.49.signal, f32[16,256]{1,0:T(8,128)S(1)} %get-tuple-element.50.weights, f32[16,8,256]{2,1,0:T(8,128)S(1)} %get-tuple-element.51.rise, f32[16,256]{1,0:T(8,128)S(1)} %get-tuple-element.47.fade, ...), custom_call_target="tpu_custom_call" | custom-call | bytes 4194304 | tf_op jit(solution)/shard_map/pallas_call | solution.py:25
  16.4 0.0 collective-permute-done.3
  16.4 1.0 %collective-permute-done.4 = f32[16,256]{1,0:T(8,128)S(1)} collective-permute-done((f32[16,256]{1,0:T(8,128)S(1)}, f32[16,256]{1,0:T(8,128)S(1)}, u32[]{:S(2)}, u32[]{:S(2)}) %collective-permute-start.4) | collective-permute-done | bytes 16416 | tf_op jit(solution)/shard_map/ppermute | solution.py:316
  17.4 0.2 collective-permute-done.5
  17.6 0.0 collective-permute-done.6
  17.7 1.3 %collective-permute-start.7 = (f32[16,256]{1,0:T(8,128)S(1)}, f32[16,256]{1,0:T(8,128)S(1)}, u32[]{:S(2)}, u32[]{:S(2)}) collective-permute-start(f32[16,256]{1,0:T(8,128)S(1)} %fusion.1), channel_id=1, source_target_pairs={{0,1},{1,0},{2,3},{3,2},{4,5},{5,4},{6,7},{7,6},{8,9},{9,8},{10,11... | collective-permute-start | bytes 49160 | tf_op jit(solution)/shard_map/ppermute | solution.py:295
  19.0 0.8 %collective-permute-done.7 = f32[16,256]{1,0:T(8,128)S(1)} collective-permute-done((f32[16,256]{1,0:T(8,128)S(1)}, f32[16,256]{1,0:T(8,128)S(1)}, u32[]{:S(2)}, u32[]{:S(2)}) %collective-permute-start.7) | collective-permute-done | bytes 16416 | tf_op jit(solution)/shard_map/ppermute | solution.py:295
  19.8 0.9 %shard_map.135 = bf16[128,256]{1,0:T(8,128)(2,1)} custom-call(f32[128,256]{1,0:T(8,128)S(1)} %get-tuple-element.58.near, f32[16,256]{1,0:T(8,128)S(1)} %fusion.carry, f32[16,8,256]{2,1,0:T(8,128)S(1)} %get-tuple-element.51.rise, f32[16,256]{1,0:T(8,128)S(1)} %get-tuple-element.47.fade, f32[128,256]{1,0:T(8,128)S(1)} %get-tuple-element.60.queries, ...), custom_call_target="tpu_custom_call" | custom-call | bytes 4194304 | tf_op jit(solution)/shard_map/pallas_call | solution.py:25
  (3 shorter events, 0.0 us)
Async XLA Ops:
  2.0 5.2 %collective-permute-start = (bf16[128,256]{1,0:T(8,128)(2,1)S(1)}, bf16[128,256]{1,0:T(8,128)(2,1)S(1)}, u32[]{:S(2)}, u32[]{:S(2)}) collective-permute-start(bf16[128,256]{1,0:T(8,128)(2,1)S(1)} %get-tuple-element.32.product), channel_id=1, source_target_pairs={{1,2},{3,4},{5,6},{7,8},{9,10},{11,12},{13,14},{4,3},{6,5},{8,7},{... | collective-permute-start | bytes 196616 | tf_op jit(solution)/shard_map/ppermute | solution.py:306
  2.5 4.7 %collective-permute-start.1 = (bf16[128,256]{1,0:T(8,128)(2,1)S(1)}, bf16[128,256]{1,0:T(8,128)(2,1)S(1)}, u32[]{:S(2)}, u32[]{:S(2)}) collective-permute-start(bf16[128,256]{1,0:T(8,128)(2,1)S(1)} %get-tuple-element.32.product), channel_id=1, source_target_pairs={{0,1},{1,0},{2,3},{3,2},{4,5},{5,4},{6,7},{7,6},{8,9},{9,8},{10,11... | collective-permute-start | bytes 196616 | tf_op jit(solution)/shard_map/ppermute | solution.py:295
  8.3 1.2 %collective-permute-start.2 = (f32[16,256]{1,0:T(8,128)S(1)}, f32[16,256]{1,0:T(8,128)S(1)}, u32[]{:S(2)}, u32[]{:S(2)}) collective-permute-start(f32[16,256]{1,0:T(8,128)S(1)} %get-tuple-element.55), channel_id=1, source_target_pairs={{0,1},{1,0},{2,3},{3,2},{4,5},{5,4},{6,7},{7,6},{8,9},{9,8},{10,11... | collective-permute-start | bytes 49160 | tf_op jit(solution)/shard_map/ppermute | solution.py:295
  9.5 6.9 %collective-permute-start.3 = (f32[16,256]{1,0:T(8,128)S(1)}, f32[16,256]{1,0:T(8,128)S(1)}, u32[]{:S(2)}, u32[]{:S(2)}) collective-permute-start(f32[16,256]{1,0:T(8,128)S(1)} %fusion.4), channel_id=1, source_target_pairs={{0,11},{1,8},{2,9},{3,10},{4,15},{5,12},{6,13},{7,14},{8,3},{9,0},... | collective-permute-start | bytes 49160 | tf_op jit(solution)/shard_map/ppermute | solution.py:316
  13.4 4.1 %collective-permute-start.4 = (f32[16,256]{1,0:T(8,128)S(1)}, f32[16,256]{1,0:T(8,128)S(1)}, u32[]{:S(2)}, u32[]{:S(2)}) collective-permute-start(f32[16,256]{1,0:T(8,128)S(1)} %fusion.4), channel_id=1, source_target_pairs={{0,15},{1,12},{2,13},{3,14},{4,11},{5,8},{6,9},{7,10},{8,3},{9,0},... | collective-permute-start | bytes 49160 | tf_op jit(solution)/shard_map/ppermute | solution.py:316
  14.4 3.2 %collective-permute-start.5 = (f32[16,256]{1,0:T(8,128)S(1)}, f32[16,256]{1,0:T(8,128)S(1)}, u32[]{:S(2)}, u32[]{:S(2)}) collective-permute-start(f32[16,256]{1,0:T(8,128)S(1)} %fusion.4), channel_id=1, source_target_pairs={{0,7},{1,4},{2,5},{3,6},{4,3},{5,0},{6,1},{7,2},{8,15},{9,12},{10,... | collective-permute-start | bytes 49160 | tf_op jit(solution)/shard_map/ppermute | solution.py:316
  14.5 3.2 %collective-permute-start.6 = (f32[16,256]{1,0:T(8,128)S(1)}, f32[16,256]{1,0:T(8,128)S(1)}, u32[]{:S(2)}, u32[]{:S(2)}) collective-permute-start(f32[16,256]{1,0:T(8,128)S(1)} %fusion.4), channel_id=1, source_target_pairs={{0,3},{1,2},{2,1},{3,0},{4,7},{5,6},{6,5},{7,4},{8,11},{9,10},{10,... | collective-permute-start | bytes 49160 | tf_op jit(solution)/shard_map/ppermute | solution.py:316
  17.7 2.2 %collective-permute-start.7 = (f32[16,256]{1,0:T(8,128)S(1)}, f32[16,256]{1,0:T(8,128)S(1)}, u32[]{:S(2)}, u32[]{:S(2)}) collective-permute-start(f32[16,256]{1,0:T(8,128)S(1)} %fusion.1), channel_id=1, source_target_pairs={{0,1},{1,0},{2,3},{3,2},{4,5},{5,4},{6,7},{7,6},{8,9},{9,8},{10,11... | collective-permute-start | bytes 49160 | tf_op jit(solution)/shard_map/ppermute | solution.py:295

commit v6 on v5

--- a/solution.py
+++ b/solution.py
@@ -107,8 +107,7 @@
 
 
 def first_kernel(
-    tokens, inv_rms, gain, proj, taps, rates, residues, inv_rms_b, gain_b,
-    product, normed, tokens_in, proj_q, taps_in, rates_in, residues_in, inv_rms_b_in, gain_b_in,
+    tokens, inv_rms, gain, proj, taps, product, normed, tokens_in, taps_in,
     proj_in, inv_rms_in, gain_in, sems,
 ):
     width = tokens.shape[1]
@@ -118,12 +117,7 @@
             (inv_rms, inv_rms_in),
             (gain, gain_in),
             (proj.at[:, width:], proj_in),
-            (proj.at[:, :width], proj_q),
             (taps, taps_in),
-            (rates, rates_in),
-            (residues, residues_in),
-            (inv_rms_b, inv_rms_b_in),
-            (gain_b, gain_b_in),
         ],
         sems,
     )
@@ -138,17 +132,32 @@
 
 
 def near_kernel(
-    devices, product, normed, proj_q, taps, rates, residues, inv_rms, gain, out_a, out_b, proj,
+    devices, product, normed, taps,
+    proj_a, rates_b, residues_b, inv_rms_b, gain_b, out_a, out_b, proj,
     total, queries, taps_wide, scale, weights, rise, fall, fade, shares, out_a_in, out_b_in, proj_in,
-    values, sems,
+    values, proj_q, rates, residues, inv_rms, gain, sems,
 ):
-    copies = fetches([(out_a, out_a_in), (proj, proj_in), (out_b, out_b_in)], sems)
+    copies = fetches(
+        [
+            (proj_a.at[:, : product.shape[1]], proj_q),
+            (rates_b, rates),
+            (residues_b, residues),
+            (inv_rms_b, inv_rms),
+            (gain_b, gain),
+            (out_a, out_a_in),
+            (proj, proj_in),
+            (out_b, out_b_in),
+        ],
+        sems,
+    )
     rows, width = product.shape
     modes = rates.shape[0]
     repeat_rows(taps[...].astype(F32), taps_wide)
     values[...] = product[...].astype(F32)
     total[...] = jnp.zeros_like(total)
     tap_sums(values, taps_wide, total, rim=False)
+    for copy in copies:
+        copy.wait()
     queries[...] = dot(normed[...], proj_q[...])
     scale[...] = spread(inv_rms[...], width) * gain[...]
     rate = rates[...]
@@ -164,12 +173,10 @@
     for i, (weighted, count, keep) in enumerate(share_plan(me, devices, rows)):
         share = jnp.exp(-rate * jnp.maximum(count, 0).astype(F32))
         shares[i] = jnp.where(keep, share * weight if weighted else share, 0.0)
-    for copy in copies:
-        copy.wait()
 
 
 def middle_kernel(
-    near, rim_chain, rim_pair, taps, queries, out_a, tokens, scale, proj, fade, fall,
+    near, rim_pair, rim_chain, taps, queries, out_a, tokens, scale, proj, fade, fall,
     partial, signal, normed_b, state, values, total,
 ):
     width = near.shape[1]
@@ -267,8 +274,7 @@
 
 
 def routes(radix):
-    pairs = {8: [(5, 4), (7, 6), (3, 2)], 4: [(3, 2)], 2: []}
-    return pairs[radix] + [(1, 1)]
+    return {8: [(5, 4), (7, 6), (3, 2)], 4: [(3, 2)], 2: []}[radix] + [(1, 1)]
 
 
 def share_plan(me, devices, rows):
@@ -278,16 +284,14 @@
     for stride, radix in levels(devices):
         place = me // stride % radix
         inner = me % stride // 2 * 2
-        last = stride * radix == devices
         for even, odd in routes(radix):
             other = place ^ jnp.where(core == 0, odd, even)
-            once = (core == 0) if even == odd else yes
             gap = ((place - 1 - other) * stride + inner) * rows
-            plan.append((False, gap, (other < place) & once))
-            if not last:
-                plan.append((False, (radix - 1 - other) * stride * rows, once))
-        if not last:
-            plan.append((False, (radix - 1 - place) * stride * rows, core == 0))
+            plan.append((False, gap, other < place))
+            if stride * radix < devices:
+                plan.append((False, (radix - 1 - other) * stride * rows, yes))
+        if stride * radix < devices:
+            plan.append((False, (radix - 1 - place) * stride * rows, yes))
     return plan + [(True, core * rows, yes), (True, 0 * core, core == 1)]
 
 
@@ -320,22 +324,26 @@
     share = iter([shares[i] for i in range(shares.shape[0])])
     beside = swap(state, devices, 1)
     total = state * next(share) + beside * next(share)
-    before = None
+    halves, wholes = [], []
     for stride, radix in levels(devices):
-        parts = [cross(total, devices, stride, radix, even, odd) for even, odd in routes(radix)]
         last = stride * radix == devices
-        sums, totals = [], []
-        for part in parts:
-            sums.append(part * next(share))
+        half_totals, whole_totals = [], []
+        pairs = routes(radix)
+        parts = [cross(total, devices, stride, radix, even, odd) for even, odd in pairs]
+        for part, (even, odd) in zip(parts, pairs):
+            (wholes if even == odd else halves).append(part * next(share))
             if not last:
-                totals.append(part * next(share))
-        half = functools.reduce(jnp.add, sums)
-        before = half if before is None else before + half
+                (whole_totals if even == odd else half_totals).append(part * next(share))
         if not last:
-            half = functools.reduce(jnp.add, totals) + total * next(share)
-            total = half + swap(half, devices, 1)
-    before, near = lax.optimization_barrier((before, near))
-    before = before + swap(before, devices, 1)
+            whole_totals.append(total * next(share))
+            total = functools.reduce(jnp.add, whole_totals)
+            if half_totals:
+                half = functools.reduce(jnp.add, half_totals)
+                total = total + half + swap(half, devices, 1)
+    if halves:
+        half, near = lax.optimization_barrier((functools.reduce(jnp.add, halves[::-1]), near))
+        wholes = [half, swap(half, devices, 1)] + wholes
+    before = functools.reduce(jnp.add, wholes)
     return before * next(share) + beside * next(share), near
 
 
@@ -368,12 +376,11 @@
     spread_taps = pltpu.VMEM((taps, SUB, width), F32)
     semaphores = pltpu.SemaphoreType.DMA
 
-    product, normed, tokens, proj_q, taps_a, rates, residues, inv_rms, gain = call(
+    product, normed, tokens, taps_a = call(
         first_kernel,
-        (narrow, narrow, narrow, square, narrow, states, states, by_token, by_channel),
-        (pltpu.VMEM((width, 2 * width), BF16), by_token, by_channel, semaphores((10,))),
-        [tokens], [inv_rms_a[None]], [gain_a[None]], [proj_a], [taps_a], [rates_b], [residues_b],
-        [inv_rms_b[None]], [gain_b[None]],
+        (narrow, narrow, narrow, pltpu.VMEM(taps_a.shape, BF16)),
+        (pltpu.VMEM((width, 2 * width), BF16), by_token, by_channel, semaphores((5,))),
+        [tokens], [inv_rms_a[None]], [gain_a[None]], [proj_a], [taps_a],
     )
     rim_chain = chain(product, devices)
     rim_pair = swap(product, devices, 1)
@@ -387,20 +394,24 @@
             wide, wide, spread_taps, wide, states, bank, bank, states, shares,
             square, square, pltpu.VMEM(proj_b.shape, BF16),
         ),
-        (wide, semaphores((3,))),
-        product, normed, proj_q, taps_a, rates, residues, inv_rms, gain, [out_a], [out_b], [proj_b],
+        (wide, square, states, states, by_token, by_channel, semaphores((8,))),
+        product, normed, taps_a, [proj_a], [rates_b], [residues_b], [inv_rms_b[None]],
+        [gain_b[None]], [out_a], [out_b], [proj_b],
     )
 
     partial_a, signal, normed_b, state = call(
         middle_kernel, (narrow, wide, narrow, states), (wide, wide),
-        near, rim_chain, rim_pair, taps_wide, queries, out_a, tokens, scale, proj_b, fade, fall,
-    )
-    near_b, queries_b, partial_a = call(
-        local_kernel,
-        (wide, wide, pltpu.HBM((rows, width), BF16)),
-        (wide, spread_taps, semaphores((1,))),
-        signal, weights, rise, fade, normed_b, proj_b, partial_a,
-    )
+        near, rim_pair, rim_chain, taps_wide, queries, out_a, tokens, scale, proj_b, fade, fall,
+    )
+    def local(signal):
+        return call(
+            local_kernel,
+            (wide, wide, pltpu.HBM((rows, width), BF16)),
+            (wide, spread_taps, semaphores((1,))),
+            signal, weights, rise, fade, normed_b, proj_b, partial_a,
+        )
+
+    near_b, queries_b, partial_a = local(signal)
     carry, near_b = carry_in(state, shares, near_b, devices)
     (partial_b,) = call(
         last_kernel, (pltpu.HBM((rows, width), BF16),), (narrow, semaphores((1,))),

time: 20.9 us -> 20.9 us (level)
  waiting for transfers between devices: 4.24 us -> 3.82 us
  Pallas kernels: 5.34 us -> 5.61 us
    ppermute x1, waiting for transfers between devices: 0.99 us -> 0.65 us  [chain(): return lax.ppermute(block, 'seq', route)]
    pallas_call x5, Pallas kernels: 5.34 us -> 5.61 us  [call(): pl.pallas_call(kernel, out_shape=outs, in_specs=[pl.BlockSpec(memory_spac...]
  transfers between devices with their start and end apart: 8 -> 8, of which waited for: 5 -> 5; matrix products, arithmetic and copies ran while one was open for 0% -> 0% of each run, Pallas kernels for 10% -> 11%
where the time goes in v6:
time: 20.9 us; the launch traced here: 20.7 us
  starting transfers between devices  10.6 us (51%)
  Pallas kernels  5.61 us (27%)
  waiting for transfers between devices  3.82 us (18%)
  between operations  0.68 us (3%)
    ppermute x4, starting transfers between devices, cross(): return lax.ppermute(block, 'seq', route)  6.04 us
    pallas_call x5, Pallas kernels, call(): pl.pallas_call(kernel, out_shape=outs, in_specs=[pl.BlockSpec(memory_spac...  5.61 us
    ppermute x3, starting transfers between devices, swap(): return lax.ppermute(block, 'seq', [(i, i ^ mask) for i in range(devices)])  4.02 us
    ppermute x3, waiting for transfers between devices, swap(): return lax.ppermute(block, 'seq', [(i, i ^ mask) for i in range(devices)])  2.01 us
    ppermute x4, waiting for transfers between devices, cross(): return lax.ppermute(block, 'seq', route)  1.16 us
    ppermute x1, waiting for transfers between devices, chain(): return lax.ppermute(block, 'seq', route)  0.65 us
    ppermute x1, starting transfers between devices, chain(): return lax.ppermute(block, 'seq', route)  0.51 us
  transfers between devices with their start and end apart: 8, of which 5 were waited for; matrix products, arithmetic and copies ran while one was open for 0% of the time, Pallas kernels for 11%

profile of v6, /device:TPU:0, one launch (start us, length us, event | category | flops | bytes accessed | tf_op | source)
XLA Modules:
  0.0 20.7 jit_solution(13478858642538918857)
XLA Ops:
  0.6 1.3 %shard_map.131 = (bf16[128,256]{1,0:T(8,128)(2,1)S(1)}, bf16[128,256]{1,0:T(8,128)(2,1)S(1)}, bf16[128,256]{1,0:T(8,128)(2,1)S(1)}, bf16[128,256]{1,0:T(8,128)(2,1)S(1)}) custom-call(bf16[128,256]{1,0:T(8,128)(2,1)} %tokens.1, f32[1,128]{1,0:T(1,128)} %bitcast.42, f32[1,256]{1,0:T(1,128)} %bitcast.40, bf16[256,768]{1,0:T(8,128)(2,1)} %proj_a.1, ...), custom_call_target="tpu_custom_call" | custom-call | bytes 4194304 | tf_op jit(solution)/shard_map/pallas_call | solution.py:25
  1.9 0.5 %collective-permute-start.1 = (bf16[128,256]{1,0:T(8,128)(2,1)S(1)}, bf16[128,256]{1,0:T(8,128)(2,1)S(1)}, u32[]{:S(2)}, u32[]{:S(2)}) collective-permute-start(bf16[128,256]{1,0:T(8,128)(2,1)S(1)} %get-tuple-element.27.product), channel_id=1, source_target_pairs={{1,2},{3,4},{5,6},{7,8},{9,10},{11,12},{13,14},{4,3},{6,5},{8,7},{... | collective-permute-start | bytes 196616 | tf_op jit(solution)/shard_map/ppermute | solution.py:310
  2.4 2.6 %collective-permute-start = (bf16[128,256]{1,0:T(8,128)(2,1)S(1)}, bf16[128,256]{1,0:T(8,128)(2,1)S(1)}, u32[]{:S(2)}, u32[]{:S(2)}) collective-permute-start(bf16[128,256]{1,0:T(8,128)(2,1)S(1)} %get-tuple-element.27.product), channel_id=1, source_target_pairs={{0,1},{1,0},{2,3},{3,2},{4,5},{5,4},{6,7},{7,6},{8,9},{9,8},{10,11... | collective-permute-start | bytes 196616 | tf_op jit(solution)/shard_map/ppermute | solution.py:299
  5.0 1.5 %shard_map.132 = (f32[128,256]{1,0:T(8,128)S(1)}, f32[128,256]{1,0:T(8,128)S(1)}, f32[128,8,256]{2,1,0:T(8,128)S(1)}, f32[128,256]{1,0:T(8,128)S(1)}, f32[16,256...) custom-call(bf16[128,256]{1,0:T(8,128)(2,1)S(1)} %get-tuple-element., ...), custom_call_target="tpu_custom_call" | custom-call | bytes 4194304 | tf_op jit(solution)/shard_map/pallas_call | solution.py:25
  6.5 0.7 %collective-permute-done.1.rim_chain = bf16[128,256]{1,0:T(8,128)(2,1)S(1)} collective-permute-done((bf16[128,256]{1,0:T(8,128)(2,1)S(1)}, bf16[128,256]{1,0:T(8,128)(2,1)S(1)}, u32[]{:S(2)}, u32[]{:S(2)}) %collective-permute-start.1) | collective-permute-done | bytes 65568 | tf_op jit(solution)/shard_map/ppermute | solution.py:310
  7.1 0.0 collective-permute-done.rim_pair
  7.1 1.1 %shard_map.133 = (bf16[128,256]{1,0:T(8,128)(2,1)S(1)}, f32[128,256]{1,0:T(8,128)S(1)}, bf16[128,256]{1,0:T(8,128)(2,1)S(1)}, f32[16,256]{1,0:T(8,128)S(1)}) custom-call(f32[128,256]{1,0:T(8,128)S(1)} %get-tuple-element.30.near, bf16[128,256]{1,0:T(8,128)(2,1)S(1)} %collective-permute-done.rim_pair, bf16[128,256]{1,0:T(8,128)(2,1)S(1)} %collective-permute-done.1.rim_chain, ...), custom_call_target="tpu_custom_call" | custom-call | bytes 4194304 | tf_op jit(solution)/shard_map/pallas_call | solution.py:25
  8.2 0.1 collective-permute-start.2
  8.3 1.2 %collective-permute-done.2 = f32[16,256]{1,0:T(8,128)S(1)} collective-permute-done((f32[16,256]{1,0:T(8,128)S(1)}, f32[16,256]{1,0:T(8,128)S(1)}, u32[]{:S(2)}, u32[]{:S(2)}) %collective-permute-start.2) | collective-permute-done | bytes 16416 | tf_op jit(solution)/shard_map/ppermute | solution.py:299
  9.5 3.8 %collective-permute-start.5 = (f32[16,256]{1,0:T(8,128)S(1)}, f32[16,256]{1,0:T(8,128)S(1)}, u32[]{:S(2)}, u32[]{:S(2)}) collective-permute-start(f32[16,256]{1,0:T(8,128)S(1)} %fusion.4), channel_id=1, source_target_pairs={{0,11},{1,8},{2,9},{3,10},{4,15},{5,12},{6,13},{7,14},{8,3},{9,0},... | collective-permute-start | bytes 49160 | tf_op jit(solution)/shard_map/ppermute | solution.py:320
  13.3 1.1 %collective-permute-start.4 = (f32[16,256]{1,0:T(8,128)S(1)}, f32[16,256]{1,0:T(8,128)S(1)}, u32[]{:S(2)}, u32[]{:S(2)}) collective-permute-start(f32[16,256]{1,0:T(8,128)S(1)} %fusion.4), channel_id=1, source_target_pairs={{0,15},{1,12},{2,13},{3,14},{4,11},{5,8},{6,9},{7,10},{8,3},{9,0},... | collective-permute-start | bytes 49160 | tf_op jit(solution)/shard_map/ppermute | solution.py:320
  14.4 0.0 collective-permute-start.3
  14.4 0.9 %shard_map.134 = (f32[128,256]{1,0:T(8,128)S(1)}, f32[128,256]{1,0:T(8,128)S(1)}, bf16[128,256]{1,0:T(8,128)(2,1)}) custom-call(f32[128,256]{1,0:T(8,128)S(1)} %get-tuple-element.39.signal, f32[16,256]{1,0:T(8,128)S(1)} %get-tuple-element.40.weights, f32[16,8,256]{2,1,0:T(8,128)S(1)} %get-tuple-element.41.rise, f32[16,256]{1,0:T(8,128)S(1)} %get-tuple-element.37.fade, ...), custom_call_target="tpu_custom_call" | custom-call | bytes 4194304 | tf_op jit(solution)/shard_map/pallas_call | solution.py:25
  15.3 1.1 %collective-permute-start.7 = (f32[16,256]{1,0:T(8,128)S(1)}, f32[16,256]{1,0:T(8,128)S(1)}, u32[]{:S(2)}, u32[]{:S(2)}) collective-permute-start(f32[16,256]{1,0:T(8,128)S(1)} %fusion.4), channel_id=1, source_target_pairs={{0,3},{1,2},{2,1},{3,0},{4,7},{5,6},{6,5},{7,4},{8,11},{9,10},{10,... | collective-permute-start | bytes 49160 | tf_op jit(solution)/shard_map/ppermute | solution.py:320
  16.4 0.0 collective-permute-done.5
  16.4 1.0 %collective-permute-done.4 = f32[16,256]{1,0:T(8,128)S(1)} collective-permute-done((f32[16,256]{1,0:T(8,128)S(1)}, f32[16,256]{1,0:T(8,128)S(1)}, u32[]{:S(2)}, u32[]{:S(2)}) %collective-permute-start.4) | collective-permute-done | bytes 16416 | tf_op jit(solution)/shard_map/ppermute | solution.py:320
  17.4 0.2 collective-permute-done.3
  17.6 1.4 %collective-permute-start.6 = (f32[16,256]{1,0:T(8,128)S(1)}, f32[16,256]{1,0:T(8,128)S(1)}, u32[]{:S(2)}, u32[]{:S(2)}) collective-permute-start(f32[16,256]{1,0:T(8,128)S(1)} %fusion.2), channel_id=1, source_target_pairs={{0,1},{1,0},{2,3},{3,2},{4,5},{5,4},{6,7},{7,6},{8,9},{9,8},{10,11... | collective-permute-start | bytes 49160 | tf_op jit(solution)/shard_map/ppermute | solution.py:299
  18.9 0.0 collective-permute-done.7
  18.9 0.8 %collective-permute-done.6 = f32[16,256]{1,0:T(8,128)S(1)} collective-permute-done((f32[16,256]{1,0:T(8,128)S(1)}, f32[16,256]{1,0:T(8,128)S(1)}, u32[]{:S(2)}, u32[]{:S(2)}) %collective-permute-start.6) | collective-permute-done | bytes 16416 | tf_op jit(solution)/shard_map/ppermute | solution.py:299
  19.8 0.9 %shard_map.135 = bf16[128,256]{1,0:T(8,128)(2,1)} custom-call(f32[128,256]{1,0:T(8,128)S(1)} %get-tuple-element.48.near, f32[16,256]{1,0:T(8,128)S(1)} %fusion.carry, f32[16,8,256]{2,1,0:T(8,128)S(1)} %get-tuple-element.41.rise, f32[16,256]{1,0:T(8,128)S(1)} %get-tuple-element.37.fade, f32[128,256]{1,0:T(8,128)S(1)} %get-tuple-element.50.queries, ...), custom_call_target="tpu_custom_call" | custom-call | bytes 4194304 | tf_op jit(solution)/shard_map/pallas_call | solution.py:25
  (3 shorter events, 0.0 us)
Async XLA Ops:
  1.9 5.2 %collective-permute-start.1 = (bf16[128,256]{1,0:T(8,128)(2,1)S(1)}, bf16[128,256]{1,0:T(8,128)(2,1)S(1)}, u32[]{:S(2)}, u32[]{:S(2)}) collective-permute-start(bf16[128,256]{1,0:T(8,128)(2,1)S(1)} %get-tuple-element.27.product), channel_id=1, source_target_pairs={{1,2},{3,4},{5,6},{7,8},{9,10},{11,12},{13,14},{4,3},{6,5},{8,7},{... | collective-permute-start | bytes 196616 | tf_op jit(solution)/shard_map/ppermute | solution.py:310
  2.4 4.7 %collective-permute-start = (bf16[128,256]{1,0:T(8,128)(2,1)S(1)}, bf16[128,256]{1,0:T(8,128)(2,1)S(1)}, u32[]{:S(2)}, u32[]{:S(2)}) collective-permute-start(bf16[128,256]{1,0:T(8,128)(2,1)S(1)} %get-tuple-element.27.product), channel_id=1, source_target_pairs={{0,1},{1,0},{2,3},{3,2},{4,5},{5,4},{6,7},{7,6},{8,9},{9,8},{10,11... | collective-permute-start | bytes 196616 | tf_op jit(solution)/shard_map/ppermute | solution.py:299
  8.2 1.2 %collective-permute-start.2 = (f32[16,256]{1,0:T(8,128)S(1)}, f32[16,256]{1,0:T(8,128)S(1)}, u32[]{:S(2)}, u32[]{:S(2)}) collective-permute-start(f32[16,256]{1,0:T(8,128)S(1)} %get-tuple-element.45), channel_id=1, source_target_pairs={{0,1},{1,0},{2,3},{3,2},{4,5},{5,4},{6,7},{7,6},{8,9},{9,8},{10,11... | collective-permute-start | bytes 49160 | tf_op jit(solution)/shard_map/ppermute | solution.py:299
  9.5 6.9 %collective-permute-start.5 = (f32[16,256]{1,0:T(8,128)S(1)}, f32[16,256]{1,0:T(8,128)S(1)}, u32[]{:S(2)}, u32[]{:S(2)}) collective-permute-start(f32[16,256]{1,0:T(8,128)S(1)} %fusion.4), channel_id=1, source_target_pairs={{0,11},{1,8},{2,9},{3,10},{4,15},{5,12},{6,13},{7,14},{8,3},{9,0},... | collective-permute-start | bytes 49160 | tf_op jit(solution)/shard_map/ppermute | solution.py:320
  13.3 4.1 %collective-permute-start.4 = (f32[16,256]{1,0:T(8,128)S(1)}, f32[16,256]{1,0:T(8,128)S(1)}, u32[]{:S(2)}, u32[]{:S(2)}) collective-permute-start(f32[16,256]{1,0:T(8,128)S(1)} %fusion.4), channel_id=1, source_target_pairs={{0,15},{1,12},{2,13},{3,14},{4,11},{5,8},{6,9},{7,10},{8,3},{9,0},... | collective-permute-start | bytes 49160 | tf_op jit(solution)/shard_map/ppermute | solution.py:320
  14.4 3.2 %collective-permute-start.3 = (f32[16,256]{1,0:T(8,128)S(1)}, f32[16,256]{1,0:T(8,128)S(1)}, u32[]{:S(2)}, u32[]{:S(2)}) collective-permute-start(f32[16,256]{1,0:T(8,128)S(1)} %fusion.4), channel_id=1, source_target_pairs={{0,7},{1,4},{2,5},{3,6},{4,3},{5,0},{6,1},{7,2},{8,15},{9,12},{10,... | collective-permute-start | bytes 49160 | tf_op jit(solution)/shard_map/ppermute | solution.py:320
  15.3 3.6 %collective-permute-start.7 = (f32[16,256]{1,0:T(8,128)S(1)}, f32[16,256]{1,0:T(8,128)S(1)}, u32[]{:S(2)}, u32[]{:S(2)}) collective-permute-start(f32[16,256]{1,0:T(8,128)S(1)} %fusion.4), channel_id=1, source_target_pairs={{0,3},{1,2},{2,1},{3,0},{4,7},{5,6},{6,5},{7,4},{8,11},{9,10},{10,... | collective-permute-start | bytes 49160 | tf_op jit(solution)/shard_map/ppermute | solution.py:320
  17.6 2.2 %collective-permute-start.6 = (f32[16,256]{1,0:T(8,128)S(1)}, f32[16,256]{1,0:T(8,128)S(1)}, u32[]{:S(2)}, u32[]{:S(2)}) collective-permute-start(f32[16,256]{1,0:T(8,128)S(1)} %fusion.2), channel_id=1, source_target_pairs={{0,1},{1,0},{2,3},{3,2},{4,5},{5,4},{6,7},{7,6},{8,9},{9,8},{10,11... | collective-permute-start | bytes 49160 | tf_op jit(solution)/shard_map/ppermute | solution.py:299

commit v7 on v5

--- a/solution.py
+++ b/solution.py
@@ -259,7 +259,7 @@
 def levels(devices):
     found, stride = [], 2
     while stride < devices:
-        radix = max(r for r in (2, 4, 8) if devices // stride % r == 0)
+        radix = 4 if stride == 2 else max(r for r in (2, 4, 8) if devices // stride % r == 0)
         found.append((stride, radix))
         stride *= radix
     assert stride == devices
@@ -267,8 +267,8 @@
 
 
 def routes(radix):
-    pairs = {8: [(5, 4), (7, 6), (3, 2)], 4: [(3, 2)], 2: []}
-    return pairs[radix] + [(1, 1)]
+    nearest = [(1, 1)]
+    return {8: [(5, 4), (7, 6), (3, 2)] + nearest, 4: nearest + [(3, 2)], 2: nearest}[radix]
 
 
 def share_plan(me, devices, rows):
@@ -278,16 +278,14 @@
     for stride, radix in levels(devices):
         place = me // stride % radix
         inner = me % stride // 2 * 2
-        last = stride * radix == devices
         for even, odd in routes(radix):
             other = place ^ jnp.where(core == 0, odd, even)
-            once = (core == 0) if even == odd else yes
             gap = ((place - 1 - other) * stride + inner) * rows
-            plan.append((False, gap, (other < place) & once))
-            if not last:
-                plan.append((False, (radix - 1 - other) * stride * rows, once))
-        if not last:
-            plan.append((False, (radix - 1 - place) * stride * rows, core == 0))
+            plan.append((False, gap, other < place))
+            if stride * radix < devices:
+                plan.append((False, (radix - 1 - other) * stride * rows, yes))
+        if stride * radix < devices:
+            plan.append((False, (radix - 1 - place) * stride * rows, yes))
     return plan + [(True, core * rows, yes), (True, 0 * core, core == 1)]
 
 
@@ -320,22 +318,26 @@
     share = iter([shares[i] for i in range(shares.shape[0])])
     beside = swap(state, devices, 1)
     total = state * next(share) + beside * next(share)
-    before = None
+    halves, wholes = [], []
     for stride, radix in levels(devices):
-        parts = [cross(total, devices, stride, radix, even, odd) for even, odd in routes(radix)]
         last = stride * radix == devices
-        sums, totals = [], []
-        for part in parts:
-            sums.append(part * next(share))
+        half_totals, whole_totals = [], []
+        pairs = routes(radix)
+        parts = [cross(total, devices, stride, radix, even, odd) for even, odd in pairs]
+        for part, (even, odd) in zip(parts, pairs):
+            (wholes if even == odd else halves).append(part * next(share))
             if not last:
-                totals.append(part * next(share))
-        half = functools.reduce(jnp.add, sums)
-        before = half if before is None else before + half
+                (whole_totals if even == odd else half_totals).append(part * next(share))
         if not last:
-            half = functools.reduce(jnp.add, totals) + total * next(share)
-            total = half + swap(half, devices, 1)
-    before, near = lax.optimization_barrier((before, near))
-    before = before + swap(before, devices, 1)
+            whole_totals.append(total * next(share))
+            total = functools.reduce(jnp.add, whole_totals)
+            if half_totals:
+                half = functools.reduce(jnp.add, half_totals)
+                total = total + half + swap(half, devices, 1)
+    if halves:
+        half, near = lax.optimization_barrier((functools.reduce(jnp.add, halves), near))
+        wholes = [half, swap(half, devices, 1)] + wholes
+    before = functools.reduce(jnp.add, wholes)
     return before * next(share) + beside * next(share), near
 
 

time: 20.9 us -> 20.9 us (level)
  starting transfers between devices: 10.5 us -> 9.6 us
  waiting for transfers between devices: 4.24 us -> 5.1 us
    ppermute x4 -> x3, waiting for transfers between devices: 1.23 us -> 2.93 us  [cross(): return lax.ppermute(block, 'seq', route)]
    ppermute x3 -> x4, waiting for transfers between devices: 2.01 us -> 1.18 us  [swap(): return lax.ppermute(block, 'seq', [(i, i ^ mask) for i in range(devices)])]
    ppermute x3 -> x4, starting transfers between devices: 4 us -> 3.25 us  [swap(): return lax.ppermute(block, 'seq', [(i, i ^ mask) for i in range(devices)])]
    ppermute x4 -> x3, starting transfers between devices: 5.97 us -> 5.85 us  [cross(): return lax.ppermute(block, 'seq', route)]
where the time goes in v7:
time: 20.9 us; the launch traced here: 20.8 us
  starting transfers between devices  9.6 us (46%)
  Pallas kernels  5.34 us (26%)
  waiting for transfers between devices  5.1 us (24%)
  between operations  0.69 us (3%)
    ppermute x3, starting transfers between devices, cross(): return lax.ppermute(block, 'seq', route)  5.85 us
    pallas_call x5, Pallas kernels, call(): pl.pallas_call(kernel, out_shape=outs, in_specs=[pl.BlockSpec(memory_spac...  5.34 us
    ppermute x4, starting transfers between devices, swap(): return lax.ppermute(block, 'seq', [(i, i ^ mask) for i in range(devices)])  3.25 us
    ppermute x3, waiting for transfers between devices, cross(): return lax.ppermute(block, 'seq', route)  2.93 us
    ppermute x4, waiting for transfers between devices, swap(): return lax.ppermute(block, 'seq', [(i, i ^ mask) for i in range(devices)])  1.18 us
    ppermute x1, waiting for transfers between devices, chain(): return lax.ppermute(block, 'seq', route)  0.99 us
    ppermute x1, starting transfers between devices, chain(): return lax.ppermute(block, 'seq', route)  0.51 us
  transfers between devices with their start and end apart: 8, of which 5 were waited for; matrix products, arithmetic and copies ran while one was open for 0% of the time, Pallas kernels for 10%

profile of v7, /device:TPU:0, one launch (start us, length us, event | category | flops | bytes accessed | tf_op | source)
XLA Modules:
  0.0 20.8 jit_solution(17246601789936142314)
XLA Ops:
  0.6 1.3 %shard_map.131 = (bf16[128,256]{1,0:T(8,128)(2,1)S(1)}, bf16[128,256]{1,0:T(8,128)(2,1)S(1)}, bf16[128,256]{1,0:T(8,128)(2,1)S(1)}, bf16[256,256]{1,0:T(8,128)(2...) custom-call(bf16[128,256]{1,0:T(8,128)(2,1)} %tokens.1, ...), custom_call_target="tpu_custom_call" | custom-call | bytes 4194304 | tf_op jit(solution)/shard_map/pallas_call | solution.py:25
  2.0 0.5 %collective-permute-start = (bf16[128,256]{1,0:T(8,128)(2,1)S(1)}, bf16[128,256]{1,0:T(8,128)(2,1)S(1)}, u32[]{:S(2)}, u32[]{:S(2)}) collective-permute-start(bf16[128,256]{1,0:T(8,128)(2,1)S(1)} %get-tuple-element.32.product), channel_id=1, source_target_pairs={{1,2},{3,4},{5,6},{7,8},{9,10},{11,12},{13,14},{4,3},{6,5},{8,7},{... | collective-permute-start | bytes 196616 | tf_op jit(solution)/shard_map/ppermute | solution.py:304
  2.5 2.6 %collective-permute-start.1 = (bf16[128,256]{1,0:T(8,128)(2,1)S(1)}, bf16[128,256]{1,0:T(8,128)(2,1)S(1)}, u32[]{:S(2)}, u32[]{:S(2)}) collective-permute-start(bf16[128,256]{1,0:T(8,128)(2,1)S(1)} %get-tuple-element.32.product), channel_id=1, source_target_pairs={{0,1},{1,0},{2,3},{3,2},{4,5},{5,4},{6,7},{7,6},{8,9},{9,8},{10,11... | collective-permute-start | bytes 196616 | tf_op jit(solution)/shard_map/ppermute | solution.py:293
  5.1 1.1 %shard_map.132 = (f32[128,256]{1,0:T(8,128)S(1)}, f32[128,256]{1,0:T(8,128)S(1)}, f32[128,8,256]{2,1,0:T(8,128)S(1)}, f32[128,256]{1,0:T(8,128)S(1)}, f32[16,256...) custom-call(bf16[128,256]{1,0:T(8,128)(2,1)S(1)} %get-tuple-element., ...), custom_call_target="tpu_custom_call" | custom-call | bytes 4194304 | tf_op jit(solution)/shard_map/pallas_call | solution.py:25
  6.2 1.0 %collective-permute-done.rim_chain = bf16[128,256]{1,0:T(8,128)(2,1)S(1)} collective-permute-done((bf16[128,256]{1,0:T(8,128)(2,1)S(1)}, bf16[128,256]{1,0:T(8,128)(2,1)S(1)}, u32[]{:S(2)}, u32[]{:S(2)}) %collective-permute-start) | collective-permute-done | bytes 65568 | tf_op jit(solution)/shard_map/ppermute | solution.py:304
  7.2 0.0 collective-permute-done.1.rim_pair
  7.2 1.1 %shard_map.133 = (bf16[128,256]{1,0:T(8,128)(2,1)S(1)}, f32[128,256]{1,0:T(8,128)S(1)}, bf16[128,256]{1,0:T(8,128)(2,1)S(1)}, f32[16,256]{1,0:T(8,128)S(1)}) custom-call(f32[128,256]{1,0:T(8,128)S(1)} %get-tuple-element.40.near, bf16[128,256]{1,0:T(8,128)(2,1)S(1)} %collective-permute-done.rim_chain, bf16[128,256]{1,0:T(8,128)(2,1)S(1)} %collective-permute-done.1.rim_pair, ...), custom_call_target="tpu_custom_call" | custom-call | bytes 4194304 | tf_op jit(solution)/shard_map/pallas_call | solution.py:25
  8.3 0.1 collective-permute-start.2
  8.3 1.2 %collective-permute-done.2 = f32[16,256]{1,0:T(8,128)S(1)} collective-permute-done((f32[16,256]{1,0:T(8,128)S(1)}, f32[16,256]{1,0:T(8,128)S(1)}, u32[]{:S(2)}, u32[]{:S(2)}) %collective-permute-start.2) | collective-permute-done | bytes 16416 | tf_op jit(solution)/shard_map/ppermute | solution.py:293
  9.5 2.8 %collective-permute-start.3 = (f32[16,256]{1,0:T(8,128)S(1)}, f32[16,256]{1,0:T(8,128)S(1)}, u32[]{:S(2)}, u32[]{:S(2)}) collective-permute-start(f32[16,256]{1,0:T(8,128)S(1)} %fusion.6), channel_id=1, source_target_pairs={{0,7},{1,4},{2,5},{3,6},{4,3},{5,0},{6,1},{7,2},{8,15},{9,12},{10,... | collective-permute-start | bytes 49160 | tf_op jit(solution)/shard_map/ppermute | solution.py:314
  12.4 0.3 %collective-permute-start.5 = (f32[16,256]{1,0:T(8,128)S(1)}, f32[16,256]{1,0:T(8,128)S(1)}, u32[]{:S(2)}, u32[]{:S(2)}) collective-permute-start(f32[16,256]{1,0:T(8,128)S(1)} %fusion.6), channel_id=1, source_target_pairs={{0,3},{1,2},{2,1},{3,0},{4,7},{5,6},{6,5},{7,4},{8,11},{9,10},{10,... | collective-permute-start | bytes 49160 | tf_op jit(solution)/shard_map/ppermute | solution.py:314
  12.6 1.2 %collective-permute-done.3 = f32[16,256]{1,0:T(8,128)S(1)} collective-permute-done((f32[16,256]{1,0:T(8,128)S(1)}, f32[16,256]{1,0:T(8,128)S(1)}, u32[]{:S(2)}, u32[]{:S(2)}) %collective-permute-start.3) | collective-permute-done | bytes 16416 | tf_op jit(solution)/shard_map/ppermute | solution.py:314
  13.8 0.1 collective-permute-start.6
  14.0 0.9 %shard_map.134 = (f32[128,256]{1,0:T(8,128)S(1)}, f32[128,256]{1,0:T(8,128)S(1)}, bf16[128,256]{1,0:T(8,128)(2,1)}) custom-call(f32[128,256]{1,0:T(8,128)S(1)} %get-tuple-element.49.signal, f32[16,256]{1,0:T(8,128)S(1)} %get-tuple-element.50.weights, f32[16,8,256]{2,1,0:T(8,128)S(1)} %get-tuple-element.51.rise, f32[16,256]{1,0:T(8,128)S(1)} %get-tuple-element.47.fade, ...), custom_call_target="tpu_custom_call" | custom-call | bytes 4194304 | tf_op jit(solution)/shard_map/pallas_call | solution.py:25
  14.9 0.4 %collective-permute-start.4 = (f32[16,256]{1,0:T(8,128)S(1)}, f32[16,256]{1,0:T(8,128)S(1)}, u32[]{:S(2)}, u32[]{:S(2)}) collective-permute-start(f32[16,256]{1,0:T(8,128)S(1)} %get-tuple-element.59), channel_id=1, source_target_pairs={{0,1},{1,0},{2,3},{3,2},{4,5},{5,4},{6,7},{7,6},{8,9},{9,8},{10,11... | collective-permute-start | bytes 49160 | tf_op jit(solution)/shard_map/ppermute | solution.py:293
  15.3 0.3 %collective-permute-done.5 = f32[16,256]{1,0:T(8,128)S(1)} collective-permute-done((f32[16,256]{1,0:T(8,128)S(1)}, f32[16,256]{1,0:T(8,128)S(1)}, u32[]{:S(2)}, u32[]{:S(2)}) %collective-permute-start.5) | collective-permute-done | bytes 16416 | tf_op jit(solution)/shard_map/ppermute | solution.py:314
  15.6 0.0 collective-permute-done.6
  15.6 2.7 %collective-permute-start.7 = (f32[16,256]{1,0:T(8,128)S(1)}, f32[16,256]{1,0:T(8,128)S(1)}, u32[]{:S(2)}, u32[]{:S(2)}) collective-permute-start(f32[16,256]{1,0:T(8,128)S(1)} %fusion.4), channel_id=1, source_target_pairs={{0,9},{1,8},{2,11},{3,10},{4,13},{5,12},{6,15},{7,14},{8,1},{9,0},... | collective-permute-start | bytes 49160 | tf_op jit(solution)/shard_map/ppermute | solution.py:314
  18.4 0.0 collective-permute-done.4
  18.4 1.4 %collective-permute-done.7 = f32[16,256]{1,0:T(8,128)S(1)} collective-permute-done((f32[16,256]{1,0:T(8,128)S(1)}, f32[16,256]{1,0:T(8,128)S(1)}, u32[]{:S(2)}, u32[]{:S(2)}) %collective-permute-start.7) | collective-permute-done | bytes 16416 | tf_op jit(solution)/shard_map/ppermute | solution.py:314
  19.8 0.9 %shard_map.135 = bf16[128,256]{1,0:T(8,128)(2,1)} custom-call(f32[128,256]{1,0:T(8,128)S(1)} %get-tuple-element.58.near, f32[16,256]{1,0:T(8,128)S(1)} %fusion.carry, f32[16,8,256]{2,1,0:T(8,128)S(1)} %get-tuple-element.51.rise, f32[16,256]{1,0:T(8,128)S(1)} %get-tuple-element.47.fade, f32[128,256]{1,0:T(8,128)S(1)} %get-tuple-element.60.queries, ...), custom_call_target="tpu_custom_call" | custom-call | bytes 4194304 | tf_op jit(solution)/shard_map/pallas_call | solution.py:25
  (4 shorter events, 0.0 us)
Async XLA Ops:
  2.0 5.2 %collective-permute-start = (bf16[128,256]{1,0:T(8,128)(2,1)S(1)}, bf16[128,256]{1,0:T(8,128)(2,1)S(1)}, u32[]{:S(2)}, u32[]{:S(2)}) collective-permute-start(bf16[128,256]{1,0:T(8,128)(2,1)S(1)} %get-tuple-element.32.product), channel_id=1, source_target_pairs={{1,2},{3,4},{5,6},{7,8},{9,10},{11,12},{13,14},{4,3},{6,5},{8,7},{... | collective-permute-start | bytes 196616 | tf_op jit(solution)/shard_map/ppermute | solution.py:304
  2.5 4.7 %collective-permute-start.1 = (bf16[128,256]{1,0:T(8,128)(2,1)S(1)}, bf16[128,256]{1,0:T(8,128)(2,1)S(1)}, u32[]{:S(2)}, u32[]{:S(2)}) collective-permute-start(bf16[128,256]{1,0:T(8,128)(2,1)S(1)} %get-tuple-element.32.product), channel_id=1, source_target_pairs={{0,1},{1,0},{2,3},{3,2},{4,5},{5,4},{6,7},{7,6},{8,9},{9,8},{10,11... | collective-permute-start | bytes 196616 | tf_op jit(solution)/shard_map/ppermute | solution.py:293
  8.3 1.2 %collective-permute-start.2 = (f32[16,256]{1,0:T(8,128)S(1)}, f32[16,256]{1,0:T(8,128)S(1)}, u32[]{:S(2)}, u32[]{:S(2)}) collective-permute-start(f32[16,256]{1,0:T(8,128)S(1)} %get-tuple-element.55), channel_id=1, source_target_pairs={{0,1},{1,0},{2,3},{3,2},{4,5},{5,4},{6,7},{7,6},{8,9},{9,8},{10,11... | collective-permute-start | bytes 49160 | tf_op jit(solution)/shard_map/ppermute | solution.py:293
  9.5 4.3 %collective-permute-start.3 = (f32[16,256]{1,0:T(8,128)S(1)}, f32[16,256]{1,0:T(8,128)S(1)}, u32[]{:S(2)}, u32[]{:S(2)}) collective-permute-start(f32[16,256]{1,0:T(8,128)S(1)} %fusion.6), channel_id=1, source_target_pairs={{0,7},{1,4},{2,5},{3,6},{4,3},{5,0},{6,1},{7,2},{8,15},{9,12},{10,... | collective-permute-start | bytes 49160 | tf_op jit(solution)/shard_map/ppermute | solution.py:314
  12.4 3.3 %collective-permute-start.5 = (f32[16,256]{1,0:T(8,128)S(1)}, f32[16,256]{1,0:T(8,128)S(1)}, u32[]{:S(2)}, u32[]{:S(2)}) collective-permute-start(f32[16,256]{1,0:T(8,128)S(1)} %fusion.6), channel_id=1, source_target_pairs={{0,3},{1,2},{2,1},{3,0},{4,7},{5,6},{6,5},{7,4},{8,11},{9,10},{10,... | collective-permute-start | bytes 49160 | tf_op jit(solution)/shard_map/ppermute | solution.py:314
  13.8 1.8 %collective-permute-start.6 = (f32[16,256]{1,0:T(8,128)S(1)}, f32[16,256]{1,0:T(8,128)S(1)}, u32[]{:S(2)}, u32[]{:S(2)}) collective-permute-start(f32[16,256]{1,0:T(8,128)S(1)} %get-tuple-element.62), channel_id=1, source_target_pairs={{0,1},{1,0},{2,3},{3,2},{4,5},{5,4},{6,7},{7,6},{8,9},{9,8},{10,11... | collective-permute-start | bytes 49160 | tf_op jit(solution)/shard_map/ppermute | solution.py:293
  14.9 3.5 %collective-permute-start.4 = (f32[16,256]{1,0:T(8,128)S(1)}, f32[16,256]{1,0:T(8,128)S(1)}, u32[]{:S(2)}, u32[]{:S(2)}) collective-permute-start(f32[16,256]{1,0:T(8,128)S(1)} %get-tuple-element.59), channel_id=1, source_target_pairs={{0,1},{1,0},{2,3},{3,2},{4,5},{5,4},{6,7},{7,6},{8,9},{9,8},{10,11... | collective-permute-start | bytes 49160 | tf_op jit(solution)/shard_map/ppermute | solution.py:293
  15.6 4.2 %collective-permute-start.7 = (f32[16,256]{1,0:T(8,128)S(1)}, f32[16,256]{1,0:T(8,128)S(1)}, u32[]{:S(2)}, u32[]{:S(2)}) collective-permute-start(f32[16,256]{1,0:T(8,128)S(1)} %fusion.4), channel_id=1, source_target_pairs={{0,9},{1,8},{2,11},{3,10},{4,13},{5,12},{6,15},{7,14},{8,1},{9,0},... | collective-permute-start | bytes 49160 | tf_op jit(solution)/shard_map/ppermute | solution.py:314
